TPU v7x, 512 devices: a whole 4x4x16 slice. The times are simulated.
512 devices in a mesh: chan: 16 (over x, y), win: 32 (over z, core).
Axes of the slice: x: 4, y: 4, z: 16, core: 2. Of those that a mesh axis runs over, the one named last changes fastest.
Arguments:
- traces: float32 [1024, 64, 1024], P('chan', 'win'), may hold values from -80 to 80, as said below
- needed: int32 [16, 48], replicated, may hold values from 0 to 1023, as said below
- home_slot: int32 [32, 8], P('chan'), may hold values from 0 to 47, as said below
- partner_slot: int32 [32, 16], P('chan'), may hold values from 0 to 47, as said below
- live_blocks: int32 [16], P('chan'), may hold values from 1 to 2, as said below
Outputs:
- correlations: float32 [4096, 1024], P(('chan', 'win'))
Inputs may be any that keep to these rules, and one draw needn't show every extreme that they name: `traces`: samples are bounded by the range. `needed`: each row lists 48 distinct channels in increasing order; row d holds exactly 6 channels of its own group d * 64 .. (d + 1) * 64 - 1 and at most 6 of any other group of 64 channels. `home_slot`: within one block the 8 home positions and 16 partner positions are all distinct. `partner_slot`: within one block the 8 home positions and 16 partner positions are all distinct. `live_blocks`: some owner uses all 2 slots and another owner uses only one.
All inputs are finite; a program needn't handle non-finite values.
Results may differ from a plain program's by a relative error of at most 0.0041.
Values may be sent and summed in bfloat16 or wider, within the bound.
No kernel may reach another device: no remote copies, remote signals or barrier semaphores. Data moves between devices by JAX's collectives and lax.ppermute only.
A program may use at most 64 MiB of HBM per device.

v0:
```python
import math

import jax
import jax.numpy as jnp
from jax import lax
from jax.sharding import PartitionSpec as P

band_reach = 64


def forward_table(samples):
    freq_bins = samples // 2
    sample_index = jnp.arange(samples, dtype=jnp.int32)[:, None]
    freq_index = jnp.arange(freq_bins, dtype=jnp.int32)[None, :]
    phase_angle = (sample_index * freq_index % samples).astype(jnp.float32) * (
        2.0 * math.pi / samples
    )
    return jnp.concatenate([jnp.cos(phase_angle), -jnp.sin(phase_angle)], axis=1)


def inverse_table(samples):
    freq_bins = samples // 2
    freq_index = jnp.arange(freq_bins, dtype=jnp.int32)[:, None]
    lag_shift = (jnp.arange(samples, dtype=jnp.int32) - samples // 2) % samples
    phase_angle = (freq_index * lag_shift[None, :] % samples).astype(jnp.float32) * (
        2.0 * math.pi / samples
    )
    weight = jnp.where(freq_index == 0, 1.0, 2.0).astype(jnp.float32)
    return jnp.concatenate([weight * jnp.cos(phase_angle), -weight * jnp.sin(phase_angle)], axis=0)


def band_table(freq_bins):
    bin_index = jnp.arange(freq_bins, dtype=jnp.int32)
    inside = (jnp.abs(bin_index[:, None] - bin_index[None, :]) <= band_reach).astype(jnp.float32)
    return inside / jnp.sum(inside, axis=0, keepdims=True)


def whiten(trace_rows):
    samples = trace_rows.shape[-1]
    freq_bins = samples // 2
    spectrum = jnp.dot(trace_rows, forward_table(samples), precision=lax.Precision.HIGHEST)
    power_bins = spectrum[:, :freq_bins] ** 2 + spectrum[:, freq_bins:] ** 2
    smooth = jnp.dot(power_bins, band_table(freq_bins), precision=lax.Precision.HIGHEST)
    factor = 1.0 / jnp.sqrt(smooth + 1e-05)
    return (spectrum * jnp.concatenate([factor, factor], axis=1)).astype(jnp.bfloat16)


def pair_product(left_side, right_side):
    return jnp.einsum("bhwf,bpwf->bhpf", left_side, right_side, preferred_element_type=jnp.float32)


def cross_spectra(home_spectra, partners):
    freq_bins = home_spectra.shape[-1] // 2
    home_re, home_im = (home_spectra[..., :freq_bins], home_spectra[..., freq_bins:])
    part_re, part_im = (partners[..., :freq_bins], partners[..., freq_bins:])
    real_part = pair_product(home_re, part_re) + pair_product(home_im, part_im)
    imag_part = pair_product(home_im, part_re) - pair_product(home_re, part_im)
    joined = jnp.concatenate([real_part, imag_part], axis=-1)
    return joined.reshape(-1, joined.shape[-1])


def body(traces, needed, home_slot, partner_slot, live_blocks):
    chan_dev, win_dev, samples = traces.shape
    groups = lax.axis_size("chan")
    win_count = lax.axis_size("win")
    owner_index = lax.axis_index("chan")
    whitened = whiten(traces.reshape(chan_dev * win_dev, samples)).reshape(
        chan_dev, win_dev, samples
    )
    listed = lax.dynamic_index_in_dim(needed, owner_index, 0, keepdims=False)
    list_length = needed.shape[1]
    capacity = 2 * list_length // groups
    first_mine = owner_index * chan_dev
    begin_at = jnp.sum((needed < first_mine).astype(jnp.int32), axis=1)
    pick_at = jnp.minimum(
        begin_at[:, None] + jnp.arange(capacity, dtype=jnp.int32)[None, :], list_length - 1
    )
    chosen = jnp.take_along_axis(needed, pick_at, axis=1)
    local_rows = jnp.clip(chosen - first_mine, 0, chan_dev - 1)
    outgoing = whitened[local_rows]
    incoming = lax.all_to_all(outgoing, "chan", split_axis=0, concat_axis=0, tiled=True)
    source = listed // chan_dev
    group_index = jnp.arange(groups, dtype=jnp.int32)
    bounds = group_index * chan_dev
    start_at = jnp.sum((listed[None, :] < bounds[:, None]).astype(jnp.int32), axis=1)
    offset = jnp.sum(
        jnp.where(source[:, None] == group_index[None, :], start_at[None, :], 0), axis=1
    )
    position = source * capacity + jnp.arange(list_length, dtype=jnp.int32) - offset
    table_rows = incoming.reshape(groups * capacity, win_dev, samples)[position]
    inverse = inverse_table(samples)
    row_share = home_slot.shape[0] * home_slot.shape[1] * partner_slot.shape[1] // win_count
    cross_terms = cross_spectra(table_rows[home_slot], table_rows[partner_slot])
    correlated = lax.psum_scatter(
        jnp.dot(cross_terms, inverse, precision=lax.Precision.HIGHEST),
        "win",
        scatter_dimension=0,
        tiled=True,
    )
    norm_scale = 1.0 / math.sqrt(samples * win_dev * win_count)
    local_index = lax.axis_index("win") * row_share + jnp.arange(row_share, dtype=jnp.int32)
    block_index = local_index // (home_slot.shape[1] * partner_slot.shape[1])
    live_mask = (block_index < live_blocks[0]).astype(jnp.float32)
    return correlated * norm_scale * live_mask[:, None]


def solution(mesh):
    placed = (P("chan", "win", None), P(), P("chan", None), P("chan", None), P("chan"))
    return jax.shard_map(
        body, mesh=mesh, in_specs=placed, out_specs=P(("chan", "win"), None), check_vma=False
    )
```

profile of v0, /device:TPU:1, one launch (start us, length us, event | category | flops | bytes accessed | tf_op | source)
XLA Modules:
  0.0 191.4 jit_solution(13933318018602789740)
XLA Ops:
  6.5 9.1 %sine_negate_fusion = (f32[1024,512]{1,0:T(8,128)S(1)}, f32[1024,512]{1,0:T(8,128)}) fusion(), kind=kLoop, calls=%fused_computation.31 | loop fusion | flops 7864320 | bytes 4194304 | tf_op jit(solution)/shard_map/neg | solution.py:18
  16.1 1.3 gather_fusion.4
  18.0 4.0 %fusion.20 = f32[128,1024]{1,0:T(8,128)S(1)} fusion(f32[128,1024]{1,0:T(8,128)S(1)} %reshape.279, f32[1024,512]{1,0:T(8,128)S(1)} %get-tuple-element.13, f32[1024,512]{1,0:T(8,128)} %get-tuple-element.14), kind=kOutput, calls=%fused_computation.38 | convolution fusion | flops 1611661312 | bytes 5242880 | tf_op jit(solution)/shard_map/dot_general | solution.py:41
  22.0 0.7 fusion.23
  22.9 2.2 %gather_fusion = bf16[96,2,1024]{2,1,0:T(2,128)(2,1)} fusion(bf16[64,2,1024]{2,1,0:T(2,128)(2,1)S(1)} %reshape.280, s32[1024]{0:T(1024)S(1)} %pad_clamp_fusion.3), kind=kCustom, calls=%fused_computation | custom fusion | bytes 786816 | tf_op jit(solution)/shard_map/gather | solution.py:80
  25.1 7.6 %all-to-all-start = ((bf16[16,6,2,1024]{3,2,1,0:T(2,128)(2,1)}), bf16[16,6,2,1024]{3,2,1,0:T(2,128)(2,1)S(1)}, u32[]{:S(2)}, u32[]{:S(2)}) async-start(bf16[16,6,2,1024]{3,2,1,0:T(2,128)(2,1)} %bitcast.1), calls=%async_computation | async-start | bytes 786432 | tf_op jit(solution)/shard_map/all_to_all | solution.py:81
  33.5 9.2 %cosine_multiply_fusion = (f32[512,1024]{1,0:T(8,128)S(1)}, f32[512,1024]{1,0:T(8,128)}) fusion(s32[1024]{0:T(1024)S(1)} %add_select_fusion.2, f32[512]{0:T(512)S(1)} %get-tuple-element.15, f32[512]{0:T(512)S(1)} %get-tuple-element.16), kind=kLoop, calls=%fused_computation.28 | loop fusion | flops 8388608 | bytes 4202496 | tf_op jit(solution)/shard_map/mul | solution.py:29
  42.7 1.0 gather_fusion.1
  43.6 0.8 gather_fusion.2
  44.5 0.4 copy.34
  44.9 0.7 gather_fusion.3
  45.6 0.4 copy.35
  46.0 1.1 copy.36
  47.1 1.1 copy.37
  48.2 1.4 fusion.47
  49.6 2.9 %fusion.48 = f32[2,512,16,8]{2,3,1,0:T(8,128)} fusion(bf16[2,16,2,512]{1,2,3,0:T(2,128)(2,1)S(1)} %copy.34, bf16[2,8,2,512]{1,2,3,0:T(2,128)(2,1)S(1)} %copy-done.4), kind=kOutput, calls=%fused_computation.105 | convolution fusion | flops 524288 | bytes 622592 | tf_op jit(solution)/shard_map/bhwf,bpwf->bhpf/dot_general | solution.py:49
  52.6 3.0 %add_bitcast_fusion = f32[2,8,16,512]{2,1,3,0:T(8,128)} fusion(f32[2,512,16,8]{2,3,1,0:T(8,128)S(1)} %fusion.47, bf16[2,16,2,512]{1,2,3,0:T(2,128)(2,1)S(1)} %copy-done.2, bf16[2,8,2,512]{1,2,3,0:T(2,128)(2,1)S(1)} %copy-done.4), kind=kOutput, calls=%fused_computation.14 | convolution fusion | flops 655360 | bytes 1146880 | tf_op jit(solution)/shard_map/bhwf,bpwf->bhpf/dot_general | solution.py:49
  55.5 3.6 %copy.32 = f32[2,8,16,512]{3,2,1,0:T(8,128)} copy(f32[2,8,16,512]{2,1,3,0:T(8,128)} %add_bitcast_fusion) | data formatting | bytes 1048576 | tf_op jit(solution)/shard_map/add | solution.py:56
  59.1 4.5 %subtract_bitcast_fusion = f32[2,8,16,512]{2,1,3,0:T(8,128)} fusion(f32[2,512,16,8]{2,3,1,0:T(8,128)} %fusion.48, bf16[2,16,2,512]{1,2,3,0:T(2,128)(2,1)S(1)} %copy-done.3, bf16[2,8,2,512]{1,2,3,0:T(2,128)(2,1)S(1)} %copy.35), kind=kOutput, calls=%fused_computation.13 | convolution fusion | flops 655360 | bytes 1146880 | tf_op jit(solution)/shard_map/bhwf,bpwf->bhpf/dot_general | solution.py:49
  63.6 2.8 %copy.33 = f32[2,8,16,512]{3,2,1,0:T(8,128)S(1)} copy(f32[2,8,16,512]{2,1,3,0:T(8,128)} %subtract_bitcast_fusion) | data formatting | bytes 1048576 | tf_op jit(solution)/shard_map/sub | solution.py:57
  66.6 1.5 copy-done.1
  68.1 4.7 %fusion.4 = f32[256,1024]{1,0:T(8,128)} fusion(f32[256,1024]{1,0:T(8,128)S(1)} %bitcast.48, f32[512,1024]{1,0:T(8,128)S(1)} %copy-done.1, f32[512,1024]{1,0:T(8,128)S(1)} %get-tuple-element.11), kind=kOutput, calls=%fused_computation.9 | convolution fusion | flops 3222274048 | bytes 6291456 | tf_op jit(solution)/shard_map/dot_general | solution.py:95
  73.5 109.7 %reduce-scatter.2.cloned.1.call-done = f32[8,1024]{1,0:T(8,128)} async-done(((f32[256,1024]{1,0:T(8,128)}), f32[8,1024]{1,0:T(8,128)}) %reduce-scatter.2.cloned.1.call-update) | async-done | bytes 32784 | tf_op jit(solution)/shard_map/reduce_scatter | solution.py:94
  183.1 1.4 broadcast_multiply_fusion
  (51 shorter events, 2.2 us)
Async XLA Ops:
  6.5 9.2 %copy-start = (s32[16,48]{1,0:T(8,128)S(1)}, s32[16,48]{1,0:T(8,128)}, u32[]{:S(2)}) copy-start(s32[16,48]{1,0:T(8,128)} %param.6) | copy-start | bytes 9220
  16.0 1.6 copy-start.6
  22.7 10.6 %copy-start.7 = (s32[2,16]{1,0:T(2,128)S(1)}, s32[2,16]{1,0:T(2,128)}, u32[]{:S(2)}) copy-start(s32[2,16]{1,0:T(2,128)} %param.8) | copy-start | bytes 388
  22.8 10.7 %copy-start.8 = (s32[2,8]{1,0:T(2,128)S(1)}, s32[2,8]{1,0:T(2,128)}, u32[]{:S(2)}) copy-start(s32[2,8]{1,0:T(2,128)} %param.7) | copy-start | bytes 196
  25.1 17.6 %all-to-all-start = ((bf16[16,6,2,1024]{3,2,1,0:T(2,128)(2,1)}), bf16[16,6,2,1024]{3,2,1,0:T(2,128)(2,1)S(1)}, u32[]{:S(2)}, u32[]{:S(2)}) async-start(bf16[16,6,2,1024]{3,2,1,0:T(2,128)(2,1)} %bitcast.1), calls=%async_computation | async-start | bytes 786432 | tf_op jit(solution)/shard_map/all_to_all | solution.py:81
  32.7 150.4 %reduce-scatter.2.cloned.1.call-start = ((), (), s32[]{:S(2)}) async-start(), calls=%async_computation.2 | async-start | bytes 1081344 | tf_op jit(solution)/shard_map/reduce_scatter | solution.py:94
  48.2 1.4 copy-start.4
  49.6 3.0 %copy-start.2 = (bf16[2,16,2,512]{1,2,3,0:T(2,128)(2,1)S(1)}, bf16[2,16,2,512]{1,2,3,0:T(2,128)(2,1)}, u32[]{:S(2)}) copy-start(bf16[2,16,2,512]{1,2,3,0:T(2,128)(2,1)} %copy.36) | copy-start | bytes 196612
  55.5 3.6 %copy-start.3 = (bf16[2,16,2,512]{1,2,3,0:T(2,128)(2,1)S(1)}, bf16[2,16,2,512]{1,2,3,0:T(2,128)(2,1)}, u32[]{:S(2)}) copy-start(bf16[2,16,2,512]{1,2,3,0:T(2,128)(2,1)} %copy.36) | copy-start | bytes 196612
  63.6 2.9 %copy-start.5 = (f32[2,8,16,512]{3,2,1,0:T(8,128)S(1)}, f32[2,8,16,512]{3,2,1,0:T(8,128)}, u32[]{:S(2)}) copy-start(f32[2,8,16,512]{3,2,1,0:T(8,128)} %copy.32) | copy-start | bytes 1572868
  66.5 1.6 copy-start.1
Sparse Core Ops, SparseCore 0:
  72.9 110.1 reduce-scatter.1
where the time goes:
time: 194 us; the launch traced here: 191 us
  waiting for transfers between devices  110 us (57%)
  matrix products  21.3 us (11%)
  other arithmetic  20.6 us (11%)
  local copies, waits for them, and re-layouts  17.7 us (9%)
  between operations  14.3 us (7%)
  starting transfers between devices  7.81 us (4%)
    reduce_scatter x1, waiting for transfers between devices, body(): lax.psum_scatter(jnp.dot(cross_terms, inverse, precision=lax.Precision.HI...  110 us
    dot_general x4, matrix products, pair_product(): jnp.einsum('bhwf,bpwf->bhpf', left_side, right_side, preferred_element_ty...  11.9 us
    mul x1, other arithmetic, inverse_table(): weight * jnp.cos(phase_angle)  9.17 us
    neg x1, other arithmetic, forward_table(): -jnp.sin(phase_angle)  9.09 us
    all_to_all x1, starting transfers between devices, body(): lax.all_to_all(outgoing, 'chan', split_axis=0, concat_axis=0, tiled=True)  7.58 us
    dot_general x1, matrix products, body(): jnp.dot(cross_terms, inverse, precision=lax.Precision.HIGHEST)  4.68 us
    unnamed x22, local copies, waits for them, and re-layouts  4.44 us
    dot_general x1, matrix products, whiten(): jnp.dot(trace_rows, forward_table(samples), precision=lax.Precision.HIGHEST)  4.01 us
  transfers between devices with their start and end apart: 2, of which 1 were waited for; matrix products, arithmetic and copies ran while one was open for 5% of the time, Pallas kernels for 0%

commit v1 on v0

v1 whole, which is shorter than its diff:
```python
import math

import jax
import jax.numpy as jnp
import ml_dtypes
import numpy as np
from jax import lax
from jax.experimental import pallas as pl
from jax.experimental.pallas import tpu as pltpu
from jax.sharding import PartitionSpec as P

band_reach = 64
F32 = jnp.float32
BF16 = jnp.bfloat16


def halves(table):
    top = table.astype(ml_dtypes.bfloat16)
    rest = (table - top.astype(np.float64)).astype(ml_dtypes.bfloat16)
    return top, rest


def bin_order(freq_bins):
    return np.concatenate([np.arange(0, freq_bins, 2), np.arange(1, freq_bins, 2)])


def forward_tables(samples):
    n = np.arange(samples // 2)[:, None]
    parts = []
    for first in (0, 1):
        k = np.arange(first, samples // 2, 2)[None, :]
        angle = (n * k % samples) * (2.0 * math.pi / samples)
        parts.append(np.concatenate([np.cos(angle), -np.sin(angle)], axis=1))
    return halves(np.stack(parts))


def inverse_tables(samples):
    lag = np.arange(samples // 2)[None, :]
    parts = []
    for first in (0, 1):
        f = np.arange(first, samples // 2, 2)[:, None]
        angle = (f * lag % samples) * (2.0 * math.pi / samples)
        weight = np.where(f == 0, 1.0, 2.0)
        parts.append(np.concatenate([weight * np.cos(angle), -weight * np.sin(angle)], axis=0))
    return halves(np.stack(parts))


def band_tables(freq_bins):
    order = bin_order(freq_bins)
    inside = np.abs(order[:, None] - order[None, :]) <= band_reach
    share = 1.0 / inside.sum(axis=0, keepdims=True)
    return inside.astype(ml_dtypes.bfloat16), share.astype(np.float32)


def split(x):
    top = x.astype(BF16)
    return top, (x - top.astype(F32)).astype(BF16)


def dot(a, b):
    return jnp.dot(a, b, preferred_element_type=F32)


def product(x, table_top, table_rest):
    rows = x.shape[0]
    top, rest = split(x)
    both = dot(jnp.concatenate([top, rest], axis=0), table_top)
    return both[:rows] + both[rows:] + dot(top, table_rest)


def one_hot(index, size):
    spots = lax.broadcasted_iota(jnp.int32, (index.shape[0], size), 1)
    return jnp.where(spots == index, 1.0, 0.0).astype(BF16)


def spectra_kernel(x_ref, top_ref, rest_ref, band_ref, share_ref, index_ref, out_ref):
    half = x_ref.shape[1] // 2
    quarter = half // 2
    left, right = x_ref[:, :half], x_ref[:, half:]
    even = product(left + right, top_ref[0], rest_ref[0])
    odd = product(left - right, top_ref[1], rest_ref[1])
    re = jnp.concatenate([even[:, :quarter], odd[:, :quarter]], axis=1)
    im = jnp.concatenate([even[:, quarter:], odd[:, quarter:]], axis=1)
    power = re * re + im * im
    rows = power.shape[0]
    top, rest = split(power)
    both = dot(jnp.concatenate([top, rest], axis=0), band_ref[...])
    smooth = (both[:rows] + both[rows:]) * share_ref[...]
    factor = 1.0 / jnp.sqrt(smooth + 1e-05)
    white = jnp.concatenate([(re * factor).astype(BF16), (im * factor).astype(BF16)], axis=0)
    out_ref[...] = dot(one_hot(index_ref[...], 2 * rows), white).astype(BF16)


def select_kernel(x_ref, index_ref, own_ref, other_ref):
    rows = own_ref.shape[0]
    picked = dot(one_hot(index_ref[...], x_ref.shape[0]), x_ref[...]).astype(BF16)
    own_ref[...] = picked[:rows]
    other_ref[...] = picked[rows:]


def cross_kernel(own_ref, other_ref, out_ref):
    for block in range(2):
        base = block * 64
        homes, partners = [], []
        for ref in (own_ref, other_ref):
            for window in range(2):
                at = base + window * 16
                homes.append(ref[at : at + 16, :].astype(F32))
                partners.append(ref[at + 32 : at + 48, :].astype(F32))
        for home in range(8):
            cr = ci = 0.0
            for a, b in zip(homes, partners):
                ar, ai = a[home : home + 1], a[home + 8 : home + 9]
                br, bi = b[:8], b[8:]
                cr = cr + (ar * br + ai * bi)
                ci = ci + (ai * br - ar * bi)
            row = (block * 8 + home) * 16
            out_ref[row : row + 16, :] = jnp.concatenate([cr, ci], axis=0).astype(BF16)


def inverse_kernel(x_ref, top_ref, rest_ref, scale_ref, out_ref):
    half = x_ref.shape[1]
    quarter = half // 2
    total = x_ref[0:16, :].astype(F32)
    for source in range(1, x_ref.shape[0] // 16):
        total = total + x_ref[source * 16 : source * 16 + 16, :].astype(F32)
    cr, ci = total[:8], total[8:]
    even = jnp.concatenate([cr[:, :quarter], ci[:, :quarter]], axis=1)
    odd = jnp.concatenate([cr[:, quarter:], ci[:, quarter:]], axis=1)
    even = product(even, top_ref[0], rest_ref[0])
    odd = product(odd, top_ref[1], rest_ref[1])
    scale = scale_ref[0]
    out_ref[:, half:] = (even + odd) * scale
    out_ref[:, :half] = (even - odd) * scale


VMEM = pl.BlockSpec(memory_space=pltpu.VMEM)
SMEM = pl.BlockSpec(memory_space=pltpu.SMEM)
PARAMS = pltpu.CompilerParams(vmem_limit_bytes=40 * 1024 * 1024)


def call(kernel, out, operands, specs=None):
    outs = out if isinstance(out, tuple) else None
    return pl.pallas_call(
        kernel,
        out_shape=out,
        in_specs=specs or [VMEM] * len(operands),
        out_specs=(VMEM,) * len(outs) if outs else VMEM,
        compiler_params=PARAMS,
    )(*operands)


def shape(rows, columns, dtype=BF16):
    return jax.ShapeDtypeStruct((rows, columns), dtype)


def body(traces, needed, home_slot, partner_slot, live_blocks):
    chan_dev, win_dev, samples = traces.shape
    bins = samples // 2
    groups = lax.axis_size("chan")
    win_count = lax.axis_size("win")
    owner = lax.axis_index("chan")
    place = lax.axis_index("win")
    core = place % 2
    length = needed.shape[1]
    capacity = 2 * length // groups
    per_group = 2 * capacity * win_dev

    first = owner * chan_dev
    begin = jnp.sum((needed < first).astype(jnp.int32), axis=1)
    listing = jnp.arange(length, dtype=jnp.int32)
    slot = jnp.arange(capacity, dtype=jnp.int32)
    hit = listing[None, None, :] == begin[:, None, None] + slot[None, :, None]
    chosen = jnp.sum(jnp.where(hit, needed[:, None, :] - first, 0), axis=2)
    part = jnp.arange(2, dtype=jnp.int32)
    send_index = (
        part[None, :, None, None] * (chan_dev * win_dev)
        + chosen[:, None, :, None] * win_dev
        + part[None, None, None, :]
    ).reshape(-1, 1)

    fore_top, fore_rest = forward_tables(samples)
    band, share = band_tables(bins)
    outgoing = call(
        spectra_kernel,
        shape(groups * per_group, bins),
        (traces.reshape(chan_dev * win_dev, samples), fore_top, fore_rest, band, share, send_index),
    )
    incoming = lax.all_to_all(
        outgoing.reshape(groups, per_group, bins), "chan", split_axis=0, concat_axis=0, tiled=True
    ).reshape(groups * per_group, bins)

    listed = lax.dynamic_index_in_dim(needed, owner, 0, keepdims=False)
    source = listed // chan_dev
    start = jnp.sum((listed[None, :] < (source * chan_dev)[:, None]).astype(jnp.int32), axis=1)
    row_of = source * per_group + (listing - start) * win_dev
    two = partner_slot.reshape(2, 2, 8)
    sides = []
    for side in (core, 1 - core):
        mine = jnp.where(side == 0, two[:, 0], two[:, 1])
        sides.append(jnp.stack([home_slot, mine], axis=1))
    slots = jnp.stack(sides)
    picked = jnp.sum(jnp.where(slots[..., None] == listing, row_of, 0), axis=-1)
    pick_index = (
        picked[:, :, :, None, None, :]
        + part[:, None, None]
        + part[None, :, None] * (capacity * win_dev)
    ).reshape(-1, 1)

    own, other = call(
        select_kernel, (shape(128, bins), shape(128, bins)), (incoming, pick_index)
    )
    received = lax.ppermute(other, "win", [(i, i ^ 1) for i in range(win_count)])
    terms = call(cross_kernel, shape(256, bins), (own, received))
    same_core = [list(range(c, win_count, 2)) for c in range(2)]
    gathered = lax.all_to_all(
        terms.reshape(16, 16, bins),
        "win",
        split_axis=0,
        concat_axis=0,
        axis_index_groups=same_core,
        tiled=True,
    ).reshape(256, bins)

    back_top, back_rest = inverse_tables(samples)
    norm_scale = 1.0 / math.sqrt(samples * win_dev * win_count)
    live = (place // (win_count // 2) < live_blocks).astype(F32) * norm_scale
    return call(
        inverse_kernel,
        shape(8, samples, F32),
        (gathered, back_top, back_rest, live),
        [VMEM, VMEM, VMEM, SMEM],
    )


def solution(mesh):
    placed = (P("chan", "win", None), P(), P("chan", None), P("chan", None), P("chan"))
    return jax.shard_map(
        body, mesh=mesh, in_specs=placed, out_specs=P(("chan", "win"), None), check_vma=False
    )
```

time: 194 us -> 62.7 us (0.32)
  the two profiles are of different devices: /device:TPU:1 before, /device:TPU:32 now
where the time goes in v1:
time: 62.7 us; the launch traced here: 62.3 us
  waiting for transfers between devices  27.9 us (44%)
  starting transfers between devices  24.3 us (39%)
  Pallas kernels  4.33 us (7%)
  local copies, waits for them, and re-layouts  3.75 us (6%)
  other arithmetic  1.15 us (2%)
  between operations  0.86 us (1%)
    all_to_all x1, waiting for transfers between devices, body(): lax.all_to_all(terms.reshape(16, 16, bins), 'win', split_axis=0, concat_a...  17.7 us
    all_to_all x1, starting transfers between devices, body(): lax.all_to_all(terms.reshape(16, 16, bins), 'win', split_axis=0, concat_a...  15.2 us
    all_to_all x1, waiting for transfers between devices, body(): lax.all_to_all(outgoing.reshape(groups, per_group, bins), 'chan', split_a...  8.91 us
    all_to_all x1, starting transfers between devices, body(): lax.all_to_all(outgoing.reshape(groups, per_group, bins), 'chan', split_a...  7.16 us
    pallas_call x4, Pallas kernels, call(): pl.pallas_call(kernel, out_shape=out, in_specs=specs or [VMEM] * len(oper...  4.33 us
    ppermute x1, starting transfers between devices, body(): lax.ppermute(other, 'win', [(i, i ^ 1) for i in range(win_count)])  1.92 us
    unnamed x18, local copies, waits for them, and re-layouts  1.87 us
    reshape x1, local copies, waits for them, and re-layouts, body(): traces.reshape(chan_dev * win_dev, samples)  1.5 us
  transfers between devices with their start and end apart: 3, of which 3 were waited for; matrix products, arithmetic and copies ran while one was open for 1% of the time, Pallas kernels for 0%

profile of v1, /device:TPU:32, one launch (start us, length us, event | category | flops | bytes accessed | tf_op | source)
XLA Modules:
  0.0 62.3 jit_solution(7991987237351312413)
XLA Ops:
  0.0 1.5 %reshape.151.x_ref = f32[128,1024]{1,0:T(8,128)S(1)} reshape(f32[64,2,1024]{2,1,0:T(2,128)} %param.11) | data formatting | bytes 1048576 | tf_op jit(solution)/shard_map/reshape | solution.py:187
  1.5 0.1 convert_reduce_fusion.1
  1.7 0.2 select_reduce_fusion
  1.9 0.1 copy.22
  2.0 0.1 broadcast_add_fusion.1
  2.1 0.1 iota_add_fusion
  2.2 0.1 add.137.index_ref
  2.3 0.3 copy-done.4
  2.6 0.4 copy-done.5
  2.9 1.2 %copy-done.1 = bf16[2,512,512]{2,1,0:T(8,128)(2,1)S(1)} copy-done((bf16[2,512,512]{2,1,0:T(8,128)(2,1)S(1)}, bf16[2,512,512]{2,1,0:T(8,128)(2,1)}, u32[]{:S(2)}) %copy-start.1) | copy-done | bytes 1048600
  4.2 1.9 %shard_map.109 = bf16[384,512]{1,0:T(8,128)(2,1)} custom-call(f32[128,1024]{1,0:T(8,128)S(1)} %reshape.151.x_ref, bf16[2,512,512]{2,1,0:T(8,128)(2,1)S(1)} %copy-done, bf16[2,512,512]{2,1,0:T(8,128)(2,1)S(1)} %copy-done.1, bf16[512,512]{1,0:T(8,128)(2,1)S(1)} %copy-done.4, f32[1,512]{1,0:T(1,128)S(1)} %copy-done.5, s32[384,1]{1,0:T(8,128)S(1)} %add.137.index_ref), custom_call_target="tpu_custom_call" | custom-call | tf_op jit(solution)/shard_map/pallas_call | solution.py:144
  6.0 7.2 %all-to-all-start = ((bf16[16,24,512]{2,1,0:T(8,128)(2,1)}), bf16[16,24,512]{2,1,0:T(8,128)(2,1)S(1)}, u32[]{:S(2)}, u32[]{:S(2)}) async-start(bf16[16,24,512]{2,1,0:T(8,128)(2,1)} %bitcast), calls=%async_computation | async-start | bytes 786432 | tf_op jit(solution)/shard_map/all_to_all | solution.py:189
  13.3 0.1 reshape.154
  13.4 0.2 convert_reduce_fusion
  13.6 0.3 select_reduce_fusion.1
  14.0 0.1 add.138.index_ref
  14.1 8.9 %all-to-all-done = bf16[16,24,512]{2,1,0:T(8,128)(2,1)S(1)} async-done(((bf16[16,24,512]{2,1,0:T(8,128)(2,1)}), bf16[16,24,512]{2,1,0:T(8,128)(2,1)S(1)}, u32[]{:S(2)}, u32[]{:S(2)}) %all-to-all-start) | async-done | bytes 393248 | tf_op jit(solution)/shard_map/all_to_all | solution.py:189
  23.0 0.3 shard_map.110
  23.4 1.9 %collective-permute-start = (bf16[128,512]{1,0:T(8,128)(2,1)S(1)}, bf16[128,512]{1,0:T(8,128)(2,1)S(1)}, u32[]{:S(2)}, u32[]{:S(2)}) collective-permute-start(bf16[128,512]{1,0:T(8,128)(2,1)S(1)} %get-tuple-element.8), channel_id=1, source_target_pairs={{0,1},{1,0},{2,3},{3,2},{4,5},{5,4},{6,7},{7,6},{8,9},{9,8},{10,11... | collective-permute-start | bytes 393224 | tf_op jit(solution)/shard_map/ppermute | solution.py:213
  25.3 1.3 %collective-permute-done.other_ref = bf16[128,512]{1,0:T(8,128)(2,1)S(1)} collective-permute-done((bf16[128,512]{1,0:T(8,128)(2,1)S(1)}, bf16[128,512]{1,0:T(8,128)(2,1)S(1)}, u32[]{:S(2)}, u32[]{:S(2)}) %collective-permute-start) | collective-permute-done | bytes 131104 | tf_op jit(solution)/shard_map/ppermute | solution.py:213
  26.6 1.1 %shard_map.111 = bf16[256,512]{1,0:T(8,128)(2,1)} custom-call(bf16[128,512]{1,0:T(8,128)(2,1)S(1)} %get-tuple-element.7.own_ref, bf16[128,512]{1,0:T(8,128)(2,1)S(1)} %collective-permute-done.other_ref), custom_call_target="tpu_custom_call" | custom-call | tf_op jit(solution)/shard_map/pallas_call | solution.py:144
  27.7 15.2 %all-to-all-start.1 = ((bf16[16,16,512]{2,1,0:T(8,128)(2,1)}), bf16[16,16,512]{2,1,0:T(8,128)(2,1)S(1)}, u32[]{:S(2)}, u32[]{:S(2)}) async-start(bf16[16,16,512]{2,1,0:T(8,128)(2,1)} %bitcast.6), calls=%async_computation.1 | async-start | bytes 524288 | tf_op jit(solution)/shard_map/all_to_all | solution.py:216
  43.6 17.7 %all-to-all-done.1 = bf16[16,16,512]{2,1,0:T(8,128)(2,1)S(1)} async-done(((bf16[16,16,512]{2,1,0:T(8,128)(2,1)}), bf16[16,16,512]{2,1,0:T(8,128)(2,1)S(1)}, u32[]{:S(2)}, u32[]{:S(2)}) %all-to-all-start.1) | async-done | bytes 262176 | tf_op jit(solution)/shard_map/all_to_all | solution.py:216
  61.3 1.0 %shard_map.112 = f32[8,1024]{1,0:T(8,128)} custom-call(bf16[256,512]{1,0:T(8,128)(2,1)S(1)} %bitcast.16, bf16[2,512,512]{2,1,0:T(8,128)(2,1)S(1)} %copy-done.2, bf16[2,512,512]{2,1,0:T(8,128)(2,1)S(1)} %copy-done.3, f32[1]{0:T(128)S(6)} %mul.64.scale_ref), custom_call_target="tpu_custom_call" | custom-call | tf_op jit(solution)/shard_map/pallas_call | solution.py:144
  (28 shorter events, 0.2 us)
Async XLA Ops:
  0.0 2.3 %copy-start = (bf16[2,512,512]{2,1,0:T(8,128)(2,1)S(1)}, bf16[2,512,512]{2,1,0:T(8,128)(2,1)}, u32[]{:S(2)}) copy-start(bf16[2,512,512]{2,1,0:T(8,128)(2,1)} %constant.83.clone.top_ref) | copy-start | bytes 3145732
  0.0 1.5 %copy-start.6 = (s32[16,48]{1,0:T(8,128)S(1)}, s32[16,48]{1,0:T(8,128)}, u32[]{:S(2)}) copy-start(s32[16,48]{1,0:T(8,128)} %param.12) | copy-start | bytes 9220
  1.5 1.0 %copy-start.4 = (bf16[512,512]{1,0:T(8,128)(2,1)S(1)}, bf16[512,512]{1,0:T(8,128)(2,1)}, u32[]{:S(2)}) copy-start(bf16[512,512]{1,0:T(8,128)(2,1)} %constant.85.clone.band_ref) | copy-start | bytes 1572868
  2.2 0.7 %copy-start.5 = (f32[1,512]{1,0:T(1,128)S(1)}, f32[1,512]{1,0:T(1,128)}, u32[]{:S(2)}) copy-start(f32[1,512]{1,0:T(1,128)} %constant.86.clone.share_ref) | copy-start | bytes 6148
  2.9 1.2 %copy-start.1 = (bf16[2,512,512]{2,1,0:T(8,128)(2,1)S(1)}, bf16[2,512,512]{2,1,0:T(8,128)(2,1)}, u32[]{:S(2)}) copy-start(bf16[2,512,512]{2,1,0:T(8,128)(2,1)} %constant.84.clone.rest_ref) | copy-start | bytes 3145732
  4.1 9.1 %copy-start.7 = (s32[2,16]{1,0:T(2,128)S(1)}, s32[2,16]{1,0:T(2,128)}, u32[]{:S(2)}) copy-start(s32[2,16]{1,0:T(2,128)} %param.14) | copy-start | bytes 388
  4.1 9.4 %copy-start.8 = (s32[2,8]{1,0:T(2,128)S(1)}, s32[2,8]{1,0:T(2,128)}, u32[]{:S(2)}) copy-start(s32[2,8]{1,0:T(2,128)} %param.13) | copy-start | bytes 196
  6.0 55.3 %copy-start.3 = (bf16[2,512,512]{2,1,0:T(8,128)(2,1)S(1)}, bf16[2,512,512]{2,1,0:T(8,128)(2,1)}, u32[]{:S(2)}) copy-start(bf16[2,512,512]{2,1,0:T(8,128)(2,1)} %constant.88.clone.rest_ref) | copy-start | bytes 3145732
  6.0 17.0 %all-to-all-start = ((bf16[16,24,512]{2,1,0:T(8,128)(2,1)}), bf16[16,24,512]{2,1,0:T(8,128)(2,1)S(1)}, u32[]{:S(2)}, u32[]{:S(2)}) async-start(bf16[16,24,512]{2,1,0:T(8,128)(2,1)} %bitcast), calls=%async_computation | async-start | bytes 786432 | tf_op jit(solution)/shard_map/all_to_all | solution.py:189
  13.2 48.1 %copy-start.2 = (bf16[2,512,512]{2,1,0:T(8,128)(2,1)S(1)}, bf16[2,512,512]{2,1,0:T(8,128)(2,1)}, u32[]{:S(2)}) copy-start(bf16[2,512,512]{2,1,0:T(8,128)(2,1)} %constant.87.clone.top_ref) | copy-start | bytes 3145732
  23.4 3.2 %collective-permute-start = (bf16[128,512]{1,0:T(8,128)(2,1)S(1)}, bf16[128,512]{1,0:T(8,128)(2,1)S(1)}, u32[]{:S(2)}, u32[]{:S(2)}) collective-permute-start(bf16[128,512]{1,0:T(8,128)(2,1)S(1)} %get-tuple-element.8), channel_id=1, source_target_pairs={{0,1},{1,0},{2,3},{3,2},{4,5},{5,4},{6,7},{7,6},{8,9},{9,8},{10,11... | collective-permute-start | bytes 393224 | tf_op jit(solution)/shard_map/ppermute | solution.py:213
  27.7 33.6 %all-to-all-start.1 = ((bf16[16,16,512]{2,1,0:T(8,128)(2,1)}), bf16[16,16,512]{2,1,0:T(8,128)(2,1)S(1)}, u32[]{:S(2)}, u32[]{:S(2)}) async-start(bf16[16,16,512]{2,1,0:T(8,128)(2,1)} %bitcast.6), calls=%async_computation.1 | async-start | bytes 524288 | tf_op jit(solution)/shard_map/all_to_all | solution.py:216

commit v2 on v1

v2 whole, which is shorter than its diff:
```python
import math

import jax
import jax.numpy as jnp
import ml_dtypes
import numpy as np
from jax import lax
from jax.experimental import pallas as pl
from jax.experimental.pallas import tpu as pltpu
from jax.sharding import PartitionSpec as P

band_reach = 64
F32 = jnp.float32
BF16 = jnp.bfloat16


def halves(table):
    top = table.astype(ml_dtypes.bfloat16)
    rest = (table - top.astype(np.float64)).astype(ml_dtypes.bfloat16)
    return top, rest


def forward_tables(samples):
    n = np.arange(samples // 2)[:, None]
    parts = []
    for first in (0, 1):
        k = np.arange(first, samples // 2, 2)[None, :]
        angle = (n * k % samples) * (2.0 * math.pi / samples)
        parts.append(np.concatenate([np.cos(angle), -np.sin(angle)], axis=1))
    return halves(np.stack(parts))


def inverse_tables(samples):
    lag = np.arange(samples // 2)[None, :]
    parts = []
    for first in (0, 1):
        f = np.arange(first, samples // 2, 2)[:, None]
        angle = (f * lag % samples) * (2.0 * math.pi / samples)
        weight = np.where(f == 0, 1.0, 2.0)
        parts.append(np.concatenate([weight * np.cos(angle), -weight * np.sin(angle)], axis=0))
    return halves(np.stack(parts))


def split(x):
    top = x.astype(BF16)
    return top, (x - top.astype(F32)).astype(BF16)


def dot(a, b):
    return jnp.dot(a, b, preferred_element_type=F32)


def product(x, table_top, table_rest):
    rows = x.shape[0]
    top, rest = split(x)
    both = dot(jnp.concatenate([top, rest], axis=0), table_top)
    return both[:rows] + both[rows:] + dot(top, table_rest)


def one_hot(index, size):
    spots = lax.broadcasted_iota(jnp.int32, (index.shape[0], size), 1)
    return jnp.where(spots == index, 1.0, 0.0).astype(BF16)


def send_rows(needed, owner, channels):
    owners, length = needed.shape
    capacity = 2 * length // owners
    per_owner = 4 * capacity
    spread = jnp.concatenate(
        [jnp.broadcast_to(needed[o : o + 1], (per_owner, length)) for o in range(owners)], axis=0
    )
    offset = spread - owner * channels
    row = lax.broadcasted_iota(jnp.int32, (owners * per_owner, 1), 0)
    row = lax.rem(row, per_owner)
    part = lax.div(row, 2 * capacity)
    slot = lax.div(lax.rem(row, 2 * capacity), 2)
    window = lax.rem(row, 2)
    begin = jnp.sum(jnp.where(offset < 0, 1.0, 0.0), axis=1, keepdims=True).astype(jnp.int32)
    at = lax.broadcasted_iota(jnp.int32, spread.shape, 1)
    chosen = jnp.where(at == begin + slot, offset, 0).astype(F32)
    chosen = jnp.sum(chosen, axis=1, keepdims=True).astype(jnp.int32)
    return part * (2 * channels) + window * channels + chosen


def band_sums(freq_bins):
    half = freq_bins // 2

    def bin_of(place):
        return jnp.where(place < half, 2 * place, 2 * place - (freq_bins - 1))

    rows = bin_of(lax.broadcasted_iota(jnp.int32, (freq_bins, freq_bins), 0))
    columns = bin_of(lax.broadcasted_iota(jnp.int32, (freq_bins, freq_bins), 1))
    inside = jnp.where(jnp.abs(rows - columns) <= band_reach, 1.0, 0.0).astype(BF16)
    k = bin_of(lax.broadcasted_iota(jnp.int32, (1, freq_bins), 1))
    count = jnp.minimum(k, band_reach) + jnp.minimum(freq_bins - 1 - k, band_reach) + 1
    return inside, 1.0 / count.astype(F32)


def spectra_kernel(owner_ref, x_hbm, table_hbm, needed_hbm, out_ref, x_ref, table_ref, needed_ref, band_ref, sems):
    channels, windows, samples = x_ref.shape
    half, quarter = samples // 2, samples // 4
    copies = [pltpu.make_async_copy(needed_hbm, needed_ref, sems.at[0])]
    for i in range(2):
        part = pl.ds(i * (channels // 2), channels // 2)
        copies.append(pltpu.make_async_copy(x_hbm.at[part], x_ref.at[part], sems.at[1 + i]))
    for i in range(8):
        part = (i // 2, pl.ds(i % 2 * quarter, quarter))
        copies.append(
            pltpu.make_async_copy(table_hbm.at[part], table_ref.at[part], sems.at[3 + i])
        )
    for copy in copies:
        copy.start()

    band, share = band_sums(half)
    band_ref[...] = band
    copies[0].wait()
    chosen = one_hot(send_rows(needed_ref[...], owner_ref[0], channels), 4 * channels)
    copies[1].wait()
    copies[2].wait()
    x = jnp.concatenate([x_ref[:, w, :] for w in range(windows)], axis=0)
    rows = x.shape[0]
    left, right = x[:, :half], x[:, half:]
    spectrum = []
    for parity, side in enumerate((left + right, left - right)):
        top, rest = split(side)
        for i in range(4):
            copies[3 + parity * 4 + i].wait()
        both = dot(jnp.concatenate([top, rest], axis=0), table_ref[2 * parity])
        spectrum.append(both[:rows] + both[rows:] + dot(top, table_ref[2 * parity + 1]))
    even, odd = spectrum
    re = jnp.concatenate([even[:, :quarter], odd[:, :quarter]], axis=1)
    im = jnp.concatenate([even[:, quarter:], odd[:, quarter:]], axis=1)
    power = re * re + im * im
    top, rest = split(power)
    both = dot(jnp.concatenate([top, rest], axis=0), band_ref[...])
    smooth = (both[:rows] + both[rows:]) * share
    factor = 1.0 / jnp.sqrt(smooth + 1e-05)
    white = jnp.concatenate([(re * factor).astype(BF16), (im * factor).astype(BF16)], axis=0)
    picked = dot(chosen, white).astype(BF16)
    width = out_ref.shape[2]
    for part in range(out_ref.shape[0]):
        out_ref[part] = picked[:, part * width : (part + 1) * width]


def cross_kernel(x_ref, index_ref, out_ref, held_ref):
    parts, rows, width = x_ref.shape
    x = jnp.concatenate([x_ref[part] for part in range(parts)], axis=1)
    held_ref[...] = dot(one_hot(index_ref[...], rows), x)
    for block in range(2):
        for home in range(8):
            cr = ci = 0.0
            for window in range(2):
                re = (block * 2 + window) * 48
                im = re + 24
                for part in range(parts):
                    lanes = slice(part * width, (part + 1) * width)
                    ar = held_ref[re + home : re + home + 1, lanes]
                    ai = held_ref[im + home : im + home + 1, lanes]
                    br = held_ref[re + 8 : re + 24, lanes]
                    bi = held_ref[im + 8 : im + 24, lanes]
                    cr = cr + (ar * br + ai * bi)
                    ci = ci + (ai * br - ar * bi)
            terms = jnp.concatenate([cr[:8], ci[:8], cr[8:], ci[8:]], axis=0)
            row = (block * 8 + home) * 32
            out_ref[row : row + 32, :] = terms.astype(BF16)


def inverse_kernel(x_ref, top_ref, rest_ref, scale_ref, out_ref):
    half = out_ref.shape[1] // 2
    re, im = [], []
    for part in range(4):
        total = 0.0
        for source in range(part, x_ref.shape[0] // 16, 4):
            total = total + x_ref[source * 16 : source * 16 + 16, :].astype(F32)
        re.append(total[:8])
        im.append(total[8:])
    even = product(jnp.concatenate(re[:2] + im[:2], axis=1), top_ref[0], rest_ref[0])
    odd = product(jnp.concatenate(re[2:] + im[2:], axis=1), top_ref[1], rest_ref[1])
    scale = scale_ref[0]
    out_ref[:, half:] = (even + odd) * scale
    out_ref[:, :half] = (even - odd) * scale


VMEM = pl.BlockSpec(memory_space=pltpu.VMEM)
SMEM = pl.BlockSpec(memory_space=pltpu.SMEM)
HBM = pl.BlockSpec(memory_space=pltpu.HBM)
MIB = 1024 * 1024


def call(kernel, out, operands, specs=None, scratch=(), vmem=32 * MIB):
    return pl.pallas_call(
        kernel,
        out_shape=out,
        in_specs=specs or [VMEM] * len(operands),
        out_specs=VMEM,
        scratch_shapes=scratch,
        compiler_params=pltpu.CompilerParams(vmem_limit_bytes=vmem),
    )(*operands)


def body(traces, needed, home_slot, partner_slot, live_blocks):
    chan_dev, win_dev, samples = traces.shape
    bins = samples // 2
    groups = lax.axis_size("chan")
    win_count = lax.axis_size("win")
    owner = lax.axis_index("chan")
    place = lax.axis_index("win")
    length = needed.shape[1]
    capacity = 2 * length // groups
    per_group = 2 * capacity * win_dev
    parts = 4
    width = bins // parts

    tops, rests = forward_tables(samples)
    table = np.stack([tops[0], rests[0], tops[1], rests[1]])
    outgoing = call(
        spectra_kernel,
        jax.ShapeDtypeStruct((parts, groups * per_group, width), BF16),
        (owner[None], traces, table, needed),
        [SMEM, HBM, HBM, HBM],
        [
            pltpu.VMEM(traces.shape, F32),
            pltpu.VMEM(table.shape, BF16),
            pltpu.VMEM(needed.shape, jnp.int32),
            pltpu.VMEM((bins, bins), BF16),
            pltpu.SemaphoreType.DMA((11,)),
        ],
        vmem=62 * MIB,
    )
    near = [
        [o * win_count + w + q for q in range(parts) for o in range(groups)]
        for w in range(0, win_count, parts)
    ]
    incoming = lax.all_to_all(
        outgoing.reshape(parts * groups, per_group, width),
        ("chan", "win"),
        split_axis=0,
        concat_axis=0,
        axis_index_groups=near,
        tiled=True,
    ).reshape(parts, groups * per_group, width)

    listing = jnp.arange(length, dtype=jnp.int32)
    listed = lax.dynamic_index_in_dim(needed, owner, 0, keepdims=False)
    source = listed // chan_dev
    start = jnp.sum((listed[None, :] < (source * chan_dev)[:, None]).astype(jnp.int32), axis=1)
    row_of = source * per_group + (listing - start) * win_dev
    slots = jnp.concatenate([home_slot, partner_slot], axis=1)
    picked = jnp.sum(jnp.where(slots[..., None] == listing, row_of, 0), axis=-1)
    part = jnp.arange(2, dtype=jnp.int32)
    pick_index = (
        picked[:, None, None, :]
        + part[None, :, None, None]
        + part[None, None, :, None] * (capacity * win_dev)
    ).reshape(-1, 1)
    terms = call(
        cross_kernel,
        jax.ShapeDtypeStruct((win_count * 16, width), BF16),
        (incoming, pick_index),
        scratch=[pltpu.VMEM((pick_index.shape[0], bins), F32)],
    )
    gathered = lax.all_to_all(
        terms.reshape(win_count, 16, width), "win", split_axis=0, concat_axis=0, tiled=True
    ).reshape(win_count * 16, width)

    back_top, back_rest = inverse_tables(samples)
    norm_scale = 1.0 / math.sqrt(samples * win_dev * win_count)
    live = (place // (win_count // 2) < live_blocks).astype(F32) * norm_scale
    return call(
        inverse_kernel,
        jax.ShapeDtypeStruct((8, samples), F32),
        (gathered, back_top, back_rest, live),
        [VMEM, VMEM, VMEM, SMEM],
    )


def solution(mesh):
    placed = (P("chan", "win", None), P(), P("chan", None), P("chan", None), P("chan"))
    return jax.shard_map(
        body, mesh=mesh, in_specs=placed, out_specs=P(("chan", "win"), None), check_vma=False
    )
```

time: 62.7 us -> 58.6 us (0.935)
  the two profiles are of different devices: /device:TPU:32 before, /device:TPU:1 now
where the time goes in v2:
time: 58.6 us; the launch traced here: 58.3 us
  starting transfers between devices  26.1 us (45%)
  waiting for transfers between devices  24.2 us (41%)
  Pallas kernels  5.92 us (10%)
  other arithmetic  1.22 us (2%)
  between operations  0.75 us (1%)
    all_to_all x1, waiting for transfers between devices, body(): lax.all_to_all(terms.reshape(win_count, 16, width), 'win', split_axis=0,...  15.2 us
    all_to_all x1, starting transfers between devices, body(): lax.all_to_all(terms.reshape(win_count, 16, width), 'win', split_axis=0,...  14.9 us
    all_to_all x1, starting transfers between devices, body(): lax.all_to_all(outgoing.reshape(parts * groups, per_group, width), ('chan...  11.2 us
    all_to_all x1, waiting for transfers between devices, body(): lax.all_to_all(outgoing.reshape(parts * groups, per_group, width), ('chan...  9.03 us
    pallas_call x3, Pallas kernels, call(): pl.pallas_call(kernel, out_shape=out, in_specs=specs or [VMEM] * len(oper...  5.92 us
  transfers between devices with their start and end apart: 2, of which 2 were waited for; matrix products, arithmetic and copies ran while one was open for 2% of the time, Pallas kernels for 0%

profile of v2, /device:TPU:1, one launch (start us, length us, event | category | flops | bytes accessed | tf_op | source)
XLA Modules:
  0.0 58.3 jit_solution(11800146753860673747)
XLA Ops:
  0.0 0.0 copy-start.2
  0.0 0.0 copy-start.3
  0.0 0.0 copy-start
  0.0 3.6 %shard_map.82 = bf16[4,384,128]{2,1,0:T(8,128)(2,1)} custom-call(s32[1]{0:T(128)} %bitcast.owner_ref, f32[64,2,1024]{2,1,0:T(2,128)} %x_hbm.1, bf16[4,512,512]{2,1,0:T(8,128)(2,1)} %constant.63.clone.table_hbm, s32[16,48]{1,0:T(8,128)} %needed_hbm.1), custom_call_target="tpu_custom_call" | custom-call | tf_op jit(solution)/shard_map/pallas_call | solution.py:191
  3.6 0.0 copy-start.1
  3.6 11.2 %all-to-all-start = ((bf16[64,24,128]{2,1,0:T(8,128)(2,1)}), bf16[64,24,128]{2,1,0:T(8,128)(2,1)S(1)}, u32[]{:S(2)}, u32[]{:S(2)}) async-start(bf16[64,24,128]{2,1,0:T(8,128)(2,1)} %bitcast.11), calls=%async_computation | async-start | bytes 786432 | tf_op jit(solution)/shard_map/all_to_all | solution.py:234
  14.8 0.0 copy-done.2
  14.8 0.0 copy-done.3
  14.9 0.1 pad_add_fusion
  14.9 0.7 %broadcast_multiply_fusion = (s32[48]{0:T(128)S(1)}, s32[48]{0:T(128)S(1)}, s32[48]{0:T(128)S(1)}) fusion(s32[16,48]{1,0:T(8,128)} %needed_hbm.1, s32[]{:T(128)S(6)} %select_n.22), kind=kLoop, calls=%fused_computation.13 | loop fusion | flops 768 | bytes 772 | tf_op jit(solution)/shard_map/mul | solution.py:246
  15.6 0.2 convert_reduce_fusion
  15.8 0.2 select_reduce_fusion
  16.0 0.1 broadcast_add_fusion
  16.1 0.1 add.63.index_ref
  16.2 9.0 %all-to-all-done = bf16[64,24,128]{2,1,0:T(8,128)(2,1)S(1)} async-done(((bf16[64,24,128]{2,1,0:T(8,128)(2,1)}), bf16[64,24,128]{2,1,0:T(8,128)(2,1)S(1)}, u32[]{:S(2)}, u32[]{:S(2)}) %all-to-all-start) | async-done | bytes 393248 | tf_op jit(solution)/shard_map/all_to_all | solution.py:234
  25.2 1.3 %shard_map.83 = bf16[512,128]{1,0:T(8,128)(2,1)} custom-call(bf16[4,384,128]{2,1,0:T(8,128)(2,1)S(1)} %bitcast.9, s32[192,1]{1,0:T(8,128)S(1)} %add.63.index_ref), custom_call_target="tpu_custom_call" | custom-call | tf_op jit(solution)/shard_map/pallas_call | solution.py:191
  26.5 14.9 %all-to-all-start.1 = ((bf16[32,16,128]{2,1,0:T(8,128)(2,1)}), bf16[32,16,128]{2,1,0:T(8,128)(2,1)S(1)}, u32[]{:S(2)}, u32[]{:S(2)}) async-start(bf16[32,16,128]{2,1,0:T(8,128)(2,1)} %bitcast.4), calls=%async_computation.1 | async-start | bytes 262144 | tf_op jit(solution)/shard_map/all_to_all | solution.py:262
  42.1 15.2 %all-to-all-done.1 = bf16[32,16,128]{2,1,0:T(8,128)(2,1)S(1)} async-done(((bf16[32,16,128]{2,1,0:T(8,128)(2,1)}), bf16[32,16,128]{2,1,0:T(8,128)(2,1)S(1)}, u32[]{:S(2)}, u32[]{:S(2)}) %all-to-all-start.1) | async-done | bytes 131104 | tf_op jit(solution)/shard_map/all_to_all | solution.py:262
  57.3 0.0 copy-done
  57.3 0.0 copy-done.1
  57.3 1.0 %shard_map.84 = f32[8,1024]{1,0:T(8,128)} custom-call(bf16[512,128]{1,0:T(8,128)(2,1)S(1)} %bitcast.10, bf16[2,512,512]{2,1,0:T(8,128)(2,1)S(1)} %copy-done, bf16[2,512,512]{2,1,0:T(8,128)(2,1)S(1)} %copy-done.1, f32[1]{0:T(128)S(6)} %mul.37.scale_ref), custom_call_target="tpu_custom_call" | custom-call | tf_op jit(solution)/shard_map/pallas_call | solution.py:191
  (3 shorter events, 0.0 us)
Async XLA Ops:
  0.0 14.8 %copy-start.2 = (s32[2,16]{1,0:T(2,128)S(1)}, s32[2,16]{1,0:T(2,128)}, u32[]{:S(2)}) copy-start(s32[2,16]{1,0:T(2,128)} %param.11) | copy-start | bytes 388
  0.0 14.8 %copy-start.3 = (s32[2,8]{1,0:T(2,128)S(1)}, s32[2,8]{1,0:T(2,128)}, u32[]{:S(2)}) copy-start(s32[2,8]{1,0:T(2,128)} %param.10) | copy-start | bytes 196
  0.0 57.3 %copy-start = (bf16[2,512,512]{2,1,0:T(8,128)(2,1)S(1)}, bf16[2,512,512]{2,1,0:T(8,128)(2,1)}, u32[]{:S(2)}) copy-start(bf16[2,512,512]{2,1,0:T(8,128)(2,1)} %constant.64.clone.top_ref) | copy-start | bytes 3145732
  3.6 53.7 %copy-start.1 = (bf16[2,512,512]{2,1,0:T(8,128)(2,1)S(1)}, bf16[2,512,512]{2,1,0:T(8,128)(2,1)}, u32[]{:S(2)}) copy-start(bf16[2,512,512]{2,1,0:T(8,128)(2,1)} %constant.65.clone.rest_ref) | copy-start | bytes 3145732
  3.6 21.6 %all-to-all-start = ((bf16[64,24,128]{2,1,0:T(8,128)(2,1)}), bf16[64,24,128]{2,1,0:T(8,128)(2,1)S(1)}, u32[]{:S(2)}, u32[]{:S(2)}) async-start(bf16[64,24,128]{2,1,0:T(8,128)(2,1)} %bitcast.11), calls=%async_computation | async-start | bytes 786432 | tf_op jit(solution)/shard_map/all_to_all | solution.py:234
  26.5 30.7 %all-to-all-start.1 = ((bf16[32,16,128]{2,1,0:T(8,128)(2,1)}), bf16[32,16,128]{2,1,0:T(8,128)(2,1)S(1)}, u32[]{:S(2)}, u32[]{:S(2)}) async-start(bf16[32,16,128]{2,1,0:T(8,128)(2,1)} %bitcast.4), calls=%async_computation.1 | async-start | bytes 262144 | tf_op jit(solution)/shard_map/all_to_all | solution.py:262

commit v3 on v2

--- a/solution.py
+++ b/solution.py
@@ -10,6 +10,8 @@
 from jax.sharding import PartitionSpec as P
 
 band_reach = 64
+first_owner = 10
+first_place = 16
 F32 = jnp.float32
 BF16 = jnp.bfloat16
 
@@ -62,12 +64,21 @@
     return jnp.where(spots == index, 1.0, 0.0).astype(BF16)
 
 
+def turned(members, first):
+    members = list(members)
+    return members[first:] + members[:first]
+
+
 def send_rows(needed, owner, channels):
     owners, length = needed.shape
     capacity = 2 * length // owners
     per_owner = 4 * capacity
     spread = jnp.concatenate(
-        [jnp.broadcast_to(needed[o : o + 1], (per_owner, length)) for o in range(owners)], axis=0
+        [
+            jnp.broadcast_to(needed[o : o + 1], (per_owner, length))
+            for o in turned(range(owners), first_owner)
+        ],
+        axis=0,
     )
     offset = spread - owner * channels
     row = lax.broadcasted_iota(jnp.int32, (owners * per_owner, 1), 0)
@@ -161,7 +172,7 @@
                     cr = cr + (ar * br + ai * bi)
                     ci = ci + (ai * br - ar * bi)
             terms = jnp.concatenate([cr[:8], ci[:8], cr[8:], ci[8:]], axis=0)
-            row = (block * 8 + home) * 32
+            row = ((block * 8 + home) * 32 - first_place * 16) % out_ref.shape[0]
             out_ref[row : row + 32, :] = terms.astype(BF16)
 
 
@@ -228,7 +239,11 @@
         vmem=62 * MIB,
     )
     near = [
-        [o * win_count + w + q for q in range(parts) for o in range(groups)]
+        [
+            o * win_count + w + q
+            for q in range(parts)
+            for o in turned(range(groups), first_owner)
+        ]
         for w in range(0, win_count, parts)
     ]
     incoming = lax.all_to_all(
@@ -244,7 +259,8 @@
     listed = lax.dynamic_index_in_dim(needed, owner, 0, keepdims=False)
     source = listed // chan_dev
     start = jnp.sum((listed[None, :] < (source * chan_dev)[:, None]).astype(jnp.int32), axis=1)
-    row_of = source * per_group + (listing - start) * win_dev
+    turn = (source - first_owner) % groups
+    row_of = turn * per_group + (listing - start) * win_dev
     slots = jnp.concatenate([home_slot, partner_slot], axis=1)
     picked = jnp.sum(jnp.where(slots[..., None] == listing, row_of, 0), axis=-1)
     part = jnp.arange(2, dtype=jnp.int32)
@@ -260,7 +276,12 @@
         scratch=[pltpu.VMEM((pick_index.shape[0], bins), F32)],
     )
     gathered = lax.all_to_all(
-        terms.reshape(win_count, 16, width), "win", split_axis=0, concat_axis=0, tiled=True
+        terms.reshape(win_count, 16, width),
+        "win",
+        split_axis=0,
+        concat_axis=0,
+        axis_index_groups=[turned(range(win_count), first_place)],
+        tiled=True,
     ).reshape(win_count * 16, width)
 
     back_top, back_rest = inverse_tables(samples)

time: 58.6 us -> 49.6 us (0.85)
  waiting for transfers between devices: 24.2 us -> 11.2 us
  starting transfers between devices: 26.1 us -> 30.1 us
    all_to_all x1, waiting for transfers between devices: 15.2 us -> 6.28 us  [body(): lax.all_to_all(terms.reshape(win_count, 16, width), 'win', split_axis=0,...]
    all_to_all x1, waiting for transfers between devices: 9.03 us -> 4.91 us  [body(): lax.all_to_all(outgoing.reshape(parts * groups, per_group, width), ('chan...]
    all_to_all x1, starting transfers between devices: 11.2 us -> 14.4 us  [body(): lax.all_to_all(outgoing.reshape(parts * groups, per_group, width), ('chan...]
    all_to_all x1, starting transfers between devices: 14.9 us -> 15.7 us  [body(): lax.all_to_all(terms.reshape(win_count, 16, width), 'win', split_axis=0,...]
  transfers between devices with their start and end apart: 2 -> 2, of which waited for: 2 -> 2; matrix products, arithmetic and copies ran while one was open for 2% -> 3% of each run, Pallas kernels for 0% -> 0%
where the time goes in v3:
time: 49.6 us; the launch traced here: 49.3 us
  starting transfers between devices  30.1 us (61%)
  waiting for transfers between devices  11.2 us (23%)
  Pallas kernels  5.92 us (12%)
  other arithmetic  1.23 us (2%)
  between operations  0.75 us (2%)
    all_to_all x1, starting transfers between devices, body(): lax.all_to_all(terms.reshape(win_count, 16, width), 'win', split_axis=0,...  15.7 us
    all_to_all x1, starting transfers between devices, body(): lax.all_to_all(outgoing.reshape(parts * groups, per_group, width), ('chan...  14.4 us
    all_to_all x1, waiting for transfers between devices, body(): lax.all_to_all(terms.reshape(win_count, 16, width), 'win', split_axis=0,...  6.28 us
    pallas_call x3, Pallas kernels, call(): pl.pallas_call(kernel, out_shape=out, in_specs=specs or [VMEM] * len(oper...  5.92 us
    all_to_all x1, waiting for transfers between devices, body(): lax.all_to_all(outgoing.reshape(parts * groups, per_group, width), ('chan...  4.91 us
  transfers between devices with their start and end apart: 2, of which 2 were waited for; matrix products, arithmetic and copies ran while one was open for 3% of the time, Pallas kernels for 0%

profile of v3, /device:TPU:1, one launch (start us, length us, event | category | flops | bytes accessed | tf_op | source)
XLA Modules:
  0.0 49.3 jit_solution(12330168697368059234)
XLA Ops:
  0.0 0.0 copy-start.2
  0.0 0.0 copy-start.3
  0.0 0.0 copy-start
  0.0 3.6 %shard_map.82 = bf16[4,384,128]{2,1,0:T(8,128)(2,1)} custom-call(s32[1]{0:T(128)} %bitcast.owner_ref, f32[64,2,1024]{2,1,0:T(2,128)} %x_hbm.1, bf16[4,512,512]{2,1,0:T(8,128)(2,1)} %constant.77.clone.table_hbm, s32[16,48]{1,0:T(8,128)} %needed_hbm.1), custom_call_target="tpu_custom_call" | custom-call | tf_op jit(solution)/shard_map/pallas_call | solution.py:202
  3.6 0.0 copy-start.1
  3.6 14.4 %all-to-all-start = ((bf16[64,24,128]{2,1,0:T(8,128)(2,1)}), bf16[64,24,128]{2,1,0:T(8,128)(2,1)S(1)}, u32[]{:S(2)}, u32[]{:S(2)}) async-start(bf16[64,24,128]{2,1,0:T(8,128)(2,1)} %bitcast.11), calls=%async_computation | async-start | bytes 786432 | tf_op jit(solution)/shard_map/all_to_all | solution.py:249
  18.1 0.0 copy-done.2
  18.1 0.0 copy-done.3
  18.1 0.1 pad_add_fusion
  18.2 0.7 %broadcast_multiply_fusion = (s32[48]{0:T(128)S(1)}, s32[48]{0:T(128)S(1)}, s32[48]{0:T(128)S(1)}) fusion(s32[16,48]{1,0:T(8,128)} %needed_hbm.1, s32[]{:T(128)S(6)} %select_n.28), kind=kLoop, calls=%fused_computation.18 | loop fusion | flops 768 | bytes 772 | tf_op jit(solution)/shard_map/mul | solution.py:261
  18.9 0.2 convert_reduce_fusion
  19.1 0.2 select_reduce_fusion
  19.3 0.1 broadcast_add_fusion
  19.4 0.1 add.71.index_ref
  19.5 4.9 %all-to-all-done = bf16[64,24,128]{2,1,0:T(8,128)(2,1)S(1)} async-done(((bf16[64,24,128]{2,1,0:T(8,128)(2,1)}), bf16[64,24,128]{2,1,0:T(8,128)(2,1)S(1)}, u32[]{:S(2)}, u32[]{:S(2)}) %all-to-all-start) | async-done | bytes 393248 | tf_op jit(solution)/shard_map/all_to_all | solution.py:249
  24.4 1.3 %shard_map.83 = bf16[512,128]{1,0:T(8,128)(2,1)} custom-call(bf16[4,384,128]{2,1,0:T(8,128)(2,1)S(1)} %bitcast.9, s32[192,1]{1,0:T(8,128)S(1)} %add.71.index_ref), custom_call_target="tpu_custom_call" | custom-call | tf_op jit(solution)/shard_map/pallas_call | solution.py:202
  25.7 15.7 %all-to-all-start.1 = ((bf16[32,16,128]{2,1,0:T(8,128)(2,1)}), bf16[32,16,128]{2,1,0:T(8,128)(2,1)S(1)}, u32[]{:S(2)}, u32[]{:S(2)}) async-start(bf16[32,16,128]{2,1,0:T(8,128)(2,1)} %bitcast.4), calls=%async_computation.1 | async-start | bytes 262144 | tf_op jit(solution)/shard_map/all_to_all | solution.py:278
  42.0 6.3 %all-to-all-done.1 = bf16[32,16,128]{2,1,0:T(8,128)(2,1)S(1)} async-done(((bf16[32,16,128]{2,1,0:T(8,128)(2,1)}), bf16[32,16,128]{2,1,0:T(8,128)(2,1)S(1)}, u32[]{:S(2)}, u32[]{:S(2)}) %all-to-all-start.1) | async-done | bytes 131104 | tf_op jit(solution)/shard_map/all_to_all | solution.py:278
  48.3 0.0 copy-done
  48.3 0.0 copy-done.1
  48.3 1.0 %shard_map.84 = f32[8,1024]{1,0:T(8,128)} custom-call(bf16[512,128]{1,0:T(8,128)(2,1)S(1)} %bitcast.10, bf16[2,512,512]{2,1,0:T(8,128)(2,1)S(1)} %copy-done, bf16[2,512,512]{2,1,0:T(8,128)(2,1)S(1)} %copy-done.1, f32[1]{0:T(128)S(6)} %mul.37.scale_ref), custom_call_target="tpu_custom_call" | custom-call | tf_op jit(solution)/shard_map/pallas_call | solution.py:202
  (3 shorter events, 0.0 us)
Async XLA Ops:
  0.0 18.1 %copy-start.2 = (s32[2,16]{1,0:T(2,128)S(1)}, s32[2,16]{1,0:T(2,128)}, u32[]{:S(2)}) copy-start(s32[2,16]{1,0:T(2,128)} %param.11) | copy-start | bytes 388
  0.0 18.1 %copy-start.3 = (s32[2,8]{1,0:T(2,128)S(1)}, s32[2,8]{1,0:T(2,128)}, u32[]{:S(2)}) copy-start(s32[2,8]{1,0:T(2,128)} %param.10) | copy-start | bytes 196
  0.0 48.3 %copy-start = (bf16[2,512,512]{2,1,0:T(8,128)(2,1)S(1)}, bf16[2,512,512]{2,1,0:T(8,128)(2,1)}, u32[]{:S(2)}) copy-start(bf16[2,512,512]{2,1,0:T(8,128)(2,1)} %constant.78.clone.top_ref) | copy-start | bytes 3145732
  3.6 44.7 %copy-start.1 = (bf16[2,512,512]{2,1,0:T(8,128)(2,1)S(1)}, bf16[2,512,512]{2,1,0:T(8,128)(2,1)}, u32[]{:S(2)}) copy-start(bf16[2,512,512]{2,1,0:T(8,128)(2,1)} %constant.79.clone.rest_ref) | copy-start | bytes 3145732
  3.6 20.7 %all-to-all-start = ((bf16[64,24,128]{2,1,0:T(8,128)(2,1)}), bf16[64,24,128]{2,1,0:T(8,128)(2,1)S(1)}, u32[]{:S(2)}, u32[]{:S(2)}) async-start(bf16[64,24,128]{2,1,0:T(8,128)(2,1)} %bitcast.11), calls=%async_computation | async-start | bytes 786432 | tf_op jit(solution)/shard_map/all_to_all | solution.py:249
  25.7 22.6 %all-to-all-start.1 = ((bf16[32,16,128]{2,1,0:T(8,128)(2,1)}), bf16[32,16,128]{2,1,0:T(8,128)(2,1)S(1)}, u32[]{:S(2)}, u32[]{:S(2)}) async-start(bf16[32,16,128]{2,1,0:T(8,128)(2,1)} %bitcast.4), calls=%async_computation.1 | async-start | bytes 262144 | tf_op jit(solution)/shard_map/all_to_all | solution.py:278

commit v4 on v3

v4 whole, which is shorter than its diff:
```python
import math

import jax
import jax.numpy as jnp
import ml_dtypes
import numpy as np
from jax import lax
from jax.experimental import pallas as pl
from jax.experimental.pallas import tpu as pltpu
from jax.sharding import PartitionSpec as P

band_reach = 64
bin_groups = (0, 2, 1, 3)
first_owner = 10
first_place = 20
F32 = jnp.float32
BF16 = jnp.bfloat16
I32 = jnp.int32


def turned(members, first):
    members = list(members)
    return members[first:] + members[:first]


def wave_tables(samples):
    n = np.arange(samples // 4)[:, None]
    parts = []
    for first in bin_groups:
        k = np.arange(first, samples // 2, 4)[None, :]
        angle = (n * k % samples) * (2.0 * math.pi / samples)
        parts.append(np.concatenate([np.cos(angle), np.sin(angle)], axis=1))
    table = np.stack(parts)
    top = table.astype(ml_dtypes.bfloat16)
    rest = (table - top.astype(np.float64)).astype(ml_dtypes.bfloat16)
    return np.stack([top, rest])


def split(x):
    top = x.astype(BF16)
    return top, (x - top.astype(F32)).astype(BF16)


def dot(a, b):
    return jnp.dot(a, b, preferred_element_type=F32)


def dot_back(a, b):
    return lax.dot_general(a, b, (((1,), (1,)), ((), ())), preferred_element_type=F32)


def product(x, table_top, table_rest, by=dot):
    rows = x.shape[0]
    top, rest = split(x)
    both = by(jnp.concatenate([top, rest], axis=0), table_top)
    return both[:rows] + both[rows:] + by(top, table_rest)


def iota(shape, axis):
    return lax.broadcasted_iota(I32, shape, axis)


def total(x, axis):
    return jnp.sum(x.astype(F32), axis=axis, keepdims=True).astype(I32)


def one_hot(index, size):
    spots = iota((index.shape[0], size), 1)
    return jnp.where(spots == index, 1.0, 0.0).astype(BF16)


def column(row):
    n = row.shape[1]
    spread = jnp.broadcast_to(row, (n, n))
    return total(jnp.where(iota((n, n), 0) == iota((n, n), 1), spread, 0), 1)


def send_rows(needed, owner, channels):
    owners, length = needed.shape
    capacity = 2 * length // owners
    per_owner = 4 * capacity
    spread = jnp.concatenate(
        [
            jnp.broadcast_to(needed[o : o + 1], (per_owner, length))
            for o in turned(range(owners), first_owner)
        ],
        axis=0,
    )
    offset = spread - owner * channels
    row = lax.rem(iota((owners * per_owner, 1), 0), per_owner)
    part = lax.div(row, 2 * capacity)
    slot = lax.div(lax.rem(row, 2 * capacity), 2)
    window = lax.rem(row, 2)
    begin = total(jnp.where(offset < 0, 1, 0), 1)
    chosen = total(jnp.where(iota(spread.shape, 1) == begin + slot, offset, 0), 1)
    return part * (2 * channels) + window * channels + chosen


def pick_rows(listed, homes, partners, owners, channels):
    length = listed.shape[1]
    capacity = 2 * length // owners
    source = lax.div(listed, channels)
    spread = jnp.broadcast_to(column(listed), (length, length))
    start = total(jnp.where(spread < source * channels, 1, 0), 0)
    turn = lax.rem(source + (owners - first_owner), owners)
    row_of = turn * (4 * capacity) + (iota((1, length), 1) - start) * 2
    rows = []
    for block in range(2):
        slots = [column(s[block : block + 1]) for s in (homes, partners)]
        slots = jnp.concatenate(slots, axis=0)
        spots = iota((slots.shape[0], length), 1)
        picked = total(jnp.where(spots == slots, row_of, 0), 1)
        for window in range(2):
            for part in range(2):
                rows.append(picked + (window + part * 2 * capacity))
    return jnp.concatenate(rows, axis=0)


def band_sums(freq_bins):
    group = freq_bins // 4

    def bin_of(place):
        at = lax.div(place, group)
        first = jnp.where(at == 1, 2, jnp.where(at == 2, 1, at))
        return 4 * lax.rem(place, group) + first

    rows = bin_of(iota((freq_bins, 1), 0))
    columns = bin_of(iota((1, freq_bins), 1))
    inside = jnp.where(jnp.abs(rows - columns) <= band_reach, 1.0, 0.0).astype(BF16)
    count = jnp.minimum(columns, band_reach) + jnp.minimum(freq_bins - 1 - columns, band_reach) + 1
    return inside, 1.0 / count.astype(F32)


def spectra_kernel(
    owner_ref, place_ref, live_ref, x_hbm, table_hbm, needed_hbm, homes_hbm, partners_hbm,
    out_ref, table_ref, pick_ref, scale_ref,
    x_ref, needed_ref, homes_ref, partners_ref, band_ref, sems,
):
    channels, windows, samples = x_ref.shape
    quarter = samples // 4
    owners = needed_ref.shape[0]
    pairs = [
        (needed_hbm, needed_ref),
        (homes_hbm, homes_ref),
        (partners_hbm, partners_ref),
    ]
    for i in range(2):
        part = pl.ds(i * (channels // 2), channels // 2)
        pairs.append((x_hbm.at[part], x_ref.at[part]))
    for group in range(4):
        for level in range(2):
            pairs.append((table_hbm.at[level, group], table_ref.at[level, group]))
    copies = [pltpu.make_async_copy(*pair, sems.at[i]) for i, pair in enumerate(pairs)]
    for copy in copies:
        copy.start()

    band, share = band_sums(samples // 2)
    band_ref[...] = band
    for copy in copies[:3]:
        copy.wait()
    chosen = one_hot(send_rows(needed_ref[...], owner_ref[0], channels), 4 * channels)
    listed = needed_ref[pl.ds(owner_ref[0], 1), :]
    pick_ref[...] = pick_rows(listed, homes_ref[...], partners_ref[...], owners, channels)
    live = lax.div(place_ref[0], 16) < live_ref[0]
    scale = jnp.where(live, 1.0 / math.sqrt(samples * 64), 0.0)
    scale_ref[...] = jnp.full(scale_ref.shape, scale, F32)

    for copy in copies[3:]:
        copy.wait()
    x = jnp.concatenate([x_ref[:, w, :] for w in range(windows)], axis=0)
    rows = x.shape[0]
    a, b, c, d = (x[:, i * quarter : (i + 1) * quarter] for i in range(4))
    ac, bd = a + c, b + d
    turns = jnp.concatenate([a - c, b - d], axis=0)
    re, im = [], []
    for group, side in enumerate((ac + bd, ac - bd, turns, turns)):
        waves = product(side, table_ref[0, group], table_ref[1, group])
        half = waves.shape[1] // 2
        cos, sin = waves[:, :half], waves[:, half:]
        if group < 2:
            re.append(cos)
            im.append(-sin)
        elif group == 2:
            re.append(cos[:rows] - sin[rows:])
            im.append(-sin[:rows] - cos[rows:])
        else:
            re.append(cos[:rows] + sin[rows:])
            im.append(cos[rows:] - sin[:rows])
    re, im = jnp.concatenate(re, axis=1), jnp.concatenate(im, axis=1)
    power = re * re + im * im
    top, rest = split(power)
    both = dot(jnp.concatenate([top, rest], axis=0), band_ref[...])
    smooth = (both[:rows] + both[rows:]) * share
    factor = 1.0 / jnp.sqrt(smooth + 1e-05)
    white = jnp.concatenate([(re * factor).astype(BF16), (im * factor).astype(BF16)], axis=0)
    picked = dot(chosen, white).astype(BF16)
    width = out_ref.shape[2]
    for part in range(out_ref.shape[0]):
        out_ref[part] = picked[:, part * width : (part + 1) * width]


def cross_kernel(x_ref, index_ref, out_ref, held_ref):
    parts, rows, width = x_ref.shape
    x = jnp.concatenate([x_ref[part] for part in range(parts)], axis=1)
    held_ref[...] = dot(one_hot(index_ref[...], rows), x)
    for block in range(2):
        cr, ci = [0.0] * 8, [0.0] * 8
        for window in range(2):
            re = (block * 2 + window) * 48
            im = re + 24
            for part in range(parts):
                lanes = slice(part * width, (part + 1) * width)
                br = held_ref[re + 8 : re + 24, lanes]
                bi = held_ref[im + 8 : im + 24, lanes]
                for home in range(8):
                    ar = held_ref[re + home : re + home + 1, lanes]
                    ai = held_ref[im + home : im + home + 1, lanes]
                    cr[home] = cr[home] + (ar * br + ai * bi)
                    ci[home] = ci[home] + (ai * br - ar * bi)
        for home in range(8):
            r, i = cr[home], ci[home]
            terms = jnp.concatenate([r[:8], i[:8], r[8:], i[8:]], axis=0)
            row = ((block * 8 + home) * 32 - first_place * 16) % out_ref.shape[0]
            out_ref[row : row + 32, :] = terms.astype(BF16)


def inverse_kernel(x_ref, table_ref, scale_ref, out_ref):
    quarter = out_ref.shape[1] // 4
    width = x_ref.shape[1]
    waves = []
    for group in range(4):
        terms = 0.0
        for source in range(group, x_ref.shape[0] // 16, 4):
            terms = terms + x_ref[source * 16 : source * 16 + 16, :].astype(F32)
        weight = 2.0
        if group == 0:
            weight = jnp.where(iota((1, width), 1) == 0, 1.0, 2.0)
        terms = terms * weight
        cr, ci = terms[:8], terms[8:]
        side = jnp.concatenate([cr, -ci], axis=1)
        if group >= 2:
            side = jnp.concatenate([side, jnp.concatenate([ci, cr], axis=1)], axis=0)
        waves.append(product(side, table_ref[0, group], table_ref[1, group], dot_back))
    a0, a2, b1, b3 = waves
    plus, minus = a0 + a2, a0 - a2
    cos = b1[:8] + b3[:8]
    sin = b1[8:] - b3[8:]
    scale = scale_ref[0:1, 0:1]
    for i, lags in enumerate((plus - cos, minus + sin, plus + cos, minus - sin)):
        out_ref[:, i * quarter : (i + 1) * quarter] = lags * scale


VMEM = pl.BlockSpec(memory_space=pltpu.VMEM)
SMEM = pl.BlockSpec(memory_space=pltpu.SMEM)
HBM = pl.BlockSpec(memory_space=pltpu.HBM)


def call(kernel, out, operands, specs=None, scratch=()):
    return pl.pallas_call(
        kernel,
        out_shape=out,
        in_specs=specs or [VMEM] * len(operands),
        out_specs=[VMEM] * len(out) if isinstance(out, list) else VMEM,
        scratch_shapes=scratch,
        compiler_params=pltpu.CompilerParams(vmem_limit_bytes=32 * 1024 * 1024),
    )(*operands)


def body(traces, needed, home_slot, partner_slot, live_blocks):
    samples = traces.shape[2]
    bins = samples // 2
    groups = lax.axis_size("chan")
    win_count = lax.axis_size("win")
    owner = lax.axis_index("chan")
    place = lax.axis_index("win")
    per_group = 8 * needed.shape[1] // groups
    parts = 4
    width = bins // parts
    held_rows = 4 * (home_slot.size + partner_slot.size)

    table = wave_tables(samples)
    far = [
        pltpu.with_memory_space_constraint(jnp.asarray(a), pltpu.HBM)
        for a in (traces, table, needed, home_slot, partner_slot)
    ]
    outgoing, waves, pick, scale = call(
        spectra_kernel,
        [
            jax.ShapeDtypeStruct((parts, groups * per_group, width), BF16),
            jax.ShapeDtypeStruct(table.shape, BF16),
            jax.ShapeDtypeStruct((held_rows, 1), I32),
            jax.ShapeDtypeStruct((8, 128), F32),
        ],
        (owner[None], place[None], live_blocks, *far),
        [SMEM, SMEM, SMEM] + [HBM] * len(far),
        [
            pltpu.VMEM(traces.shape, F32),
            pltpu.VMEM(needed.shape, I32),
            pltpu.VMEM(home_slot.shape, I32),
            pltpu.VMEM(partner_slot.shape, I32),
            pltpu.VMEM((bins, bins), BF16),
            pltpu.SemaphoreType.DMA((13,)),
        ],
    )
    near = [
        [
            o * win_count + w + q
            for q in range(parts)
            for o in turned(range(groups), first_owner)
        ]
        for w in range(0, win_count, parts)
    ]
    incoming = lax.all_to_all(
        outgoing.reshape(parts * groups, per_group, width),
        ("chan", "win"),
        split_axis=0,
        concat_axis=0,
        axis_index_groups=near,
        tiled=True,
    ).reshape(parts, groups * per_group, width)
    terms = call(
        cross_kernel,
        jax.ShapeDtypeStruct((win_count * 16, width), BF16),
        (incoming, pick),
        scratch=[pltpu.VMEM((held_rows, bins), F32)],
    )
    gathered = lax.all_to_all(
        terms.reshape(win_count, 16, width),
        "win",
        split_axis=0,
        concat_axis=0,
        axis_index_groups=[turned(range(win_count), first_place)],
        tiled=True,
    ).reshape(win_count * 16, width)
    return call(
        inverse_kernel, jax.ShapeDtypeStruct((8, samples), F32), (gathered, waves, scale)
    )


def solution(mesh):
    placed = (P("chan", "win", None), P(), P("chan", None), P("chan", None), P("chan"))
    return jax.shard_map(
        body, mesh=mesh, in_specs=placed, out_specs=P(("chan", "win"), None), check_vma=False
    )
```

time: 49.6 us -> 47.9 us (0.966)
  blocking collectives: 0 us -> 42.7 us
  starting transfers between devices: 30.1 us -> 0 us
  waiting for transfers between devices: 11.2 us -> 0 us
  Pallas kernels: 5.92 us -> 4.34 us
  other arithmetic: 1.23 us -> 0 us
    all_to_all x0 -> x2, blocking collectives: none -> 42.7 us  [the longest x1 22.3 us: body(): lax.all_to_all(terms.reshape(win_count, 16, width), 'win', split_axis=0,...]
    all_to_all x2 -> x0, starting transfers between devices: 30.1 us -> none  [the longest x1 15.7 us: body(): lax.all_to_all(terms.reshape(win_count, 16, width), 'win', split_axis=0,...]
    all_to_all x2 -> x0, waiting for transfers between devices: 11.2 us -> none  [the longest x1 6.28 us: body(): lax.all_to_all(terms.reshape(win_count, 16, width), 'win', split_axis=0,...]
    pallas_call x3, Pallas kernels: 5.92 us -> 4.34 us  [call(): pl.pallas_call(kernel, out_shape=out, in_specs=specs or [VMEM] * len(oper...]
    mul x2 -> x0, other arithmetic: 0.7 us -> none  [the longest x1 0.7 us: body(): source * chan_dev]
  transfers between devices with their start and end apart: 2 -> 0, of which waited for: 2 -> 0; matrix products, arithmetic and copies ran while one was open for 3% -> 0% of each run, Pallas kernels for 0% -> 0%
where the time goes in v4:
time: 47.9 us; the launch traced here: 47.7 us
  blocking collectives  42.7 us (89%)
  Pallas kernels  4.34 us (9%)
  between operations  0.67 us (1%)
    all_to_all x1, blocking collectives, body(): lax.all_to_all(terms.reshape(win_count, 16, width), 'win', split_axis=0,...  22.3 us
    all_to_all x1, blocking collectives, body(): lax.all_to_all(outgoing.reshape(parts * groups, per_group, width), ('chan...  20.4 us
    pallas_call x3, Pallas kernels, call(): pl.pallas_call(kernel, out_shape=out, in_specs=specs or [VMEM] * len(oper...  4.34 us

profile of v4, /device:TPU:1, one launch (start us, length us, event | category | flops | bytes accessed | tf_op | source)
XLA Modules:
  0.0 47.7 jit_solution(6876189875680211837)
XLA Ops:
  0.7 2.6 %shard_map.64 = (bf16[4,384,128]{2,1,0:T(8,128)(2,1)S(1)}, bf16[2,4,256,256]{3,2,1,0:T(8,128)(2,1)S(1)}, s32[192,1]{1,0:T(8,128)S(1)}, f32[8,128]{1,0:T(8,128)S(1)}) custom-call(s32[1]{0:T(128)} %bitcast.owner_ref, s32[1]{0:T(128)} %bitcast.1.place_ref, s32[1]{0:T(128)S(6)} %copy.7.live_ref, f32[64,2,1024]{2,1,0:T(2,128)} %x_hbm.1, ...), custom_call_target="tpu_custom_call" | custom-call | tf_op jit(solution)/shard_map/pallas_call | solution.py:259
  3.3 20.4 %all_to_all.10 = bf16[64,24,128]{2,1,0:T(8,128)(2,1)S(1)} all-to-all(bf16[64,24,128]{2,1,0:T(8,128)(2,1)S(1)} %bitcast.9), channel_id=1, replica_groups={{320,352,384,416,448,480,0,32,64,96,128,160,192,224,256,288,321,353,385..., dimensions={0} | all-to-all | bytes 786432 | tf_op jit(solution)/shard_map/all_to_all | solution.py:313
  23.7 0.7 %shard_map.65 = bf16[512,128]{1,0:T(8,128)(2,1)S(1)} custom-call(bf16[4,384,128]{2,1,0:T(8,128)(2,1)S(1)} %bitcast.6, s32[192,1]{1,0:T(8,128)S(1)} %get-tuple-element.10.index_ref), custom_call_target="tpu_custom_call" | custom-call | tf_op jit(solution)/shard_map/pallas_call | solution.py:259
  24.4 22.3 %all_to_all.11 = bf16[32,16,128]{2,1,0:T(8,128)(2,1)S(1)} all-to-all(bf16[32,16,128]{2,1,0:T(8,128)(2,1)S(1)} %bitcast.8), channel_id=1, replica_groups={{20,21,22,23,24,25,26,27,28,29,30,31,0,1,2,3,4,5,6,7,8,9,10,11,12,13,14..., dimensions={0} | all-to-all | bytes 262144 | tf_op jit(solution)/shard_map/all_to_all | solution.py:327
  46.7 1.0 %shard_map.66 = f32[8,1024]{1,0:T(8,128)} custom-call(bf16[512,128]{1,0:T(8,128)(2,1)S(1)} %bitcast.7, bf16[2,4,256,256]{3,2,1,0:T(8,128)(2,1)S(1)} %get-tuple-element.11.table_ref, f32[8,128]{1,0:T(8,128)S(1)} %get-tuple-element.12.scale_ref), custom_call_target="tpu_custom_call" | custom-call | tf_op jit(solution)/shard_map/pallas_call | solution.py:259

commit v5 on v4

--- a/solution.py
+++ b/solution.py
@@ -11,16 +11,11 @@
 
 band_reach = 64
 bin_groups = (0, 2, 1, 3)
-first_owner = 10
-first_place = 20
+owner_order = tuple((10 + i) % 16 for i in range(16))
+place_order = (20, 21, 2, 3, 16, 17, 30, 31, 12, 13, 26, 27, 8, 9, 22, 23, 4, 5, 18, 19, 0, 1, 14, 15, 28, 29, 10, 11, 24, 25, 6, 7)
 F32 = jnp.float32
 BF16 = jnp.bfloat16
 I32 = jnp.int32
-
-
-def turned(members, first):
-    members = list(members)
-    return members[first:] + members[:first]
 
 
 def wave_tables(samples):
@@ -82,7 +77,7 @@
     spread = jnp.concatenate(
         [
             jnp.broadcast_to(needed[o : o + 1], (per_owner, length))
-            for o in turned(range(owners), first_owner)
+            for o in owner_order
         ],
         axis=0,
     )
@@ -102,7 +97,9 @@
     source = lax.div(listed, channels)
     spread = jnp.broadcast_to(column(listed), (length, length))
     start = total(jnp.where(spread < source * channels, 1, 0), 0)
-    turn = lax.rem(source + (owners - first_owner), owners)
+    turn = 0
+    for spot, owner in enumerate(owner_order):
+        turn = jnp.where(source == owner, spot, turn)
     row_of = turn * (4 * capacity) + (iota((1, length), 1) - start) * 2
     rows = []
     for block in range(2):
@@ -191,7 +188,7 @@
     top, rest = split(power)
     both = dot(jnp.concatenate([top, rest], axis=0), band_ref[...])
     smooth = (both[:rows] + both[rows:]) * share
-    factor = 1.0 / jnp.sqrt(smooth + 1e-05)
+    factor = lax.rsqrt(smooth + 1e-05)
     white = jnp.concatenate([(re * factor).astype(BF16), (im * factor).astype(BF16)], axis=0)
     picked = dot(chosen, white).astype(BF16)
     width = out_ref.shape[2]
@@ -220,8 +217,10 @@
         for home in range(8):
             r, i = cr[home], ci[home]
             terms = jnp.concatenate([r[:8], i[:8], r[8:], i[8:]], axis=0)
-            row = ((block * 8 + home) * 32 - first_place * 16) % out_ref.shape[0]
-            out_ref[row : row + 32, :] = terms.astype(BF16)
+            terms = terms.astype(BF16)
+            for side in range(2):
+                row = place_order.index((block * 8 + home) * 2 + side) * 16
+                out_ref[row : row + 16, :] = terms[side * 16 : side * 16 + 16]
 
 
 def inverse_kernel(x_ref, table_ref, scale_ref, out_ref):
@@ -230,7 +229,9 @@
     waves = []
     for group in range(4):
         terms = 0.0
-        for source in range(group, x_ref.shape[0] // 16, 4):
+        for source, place in enumerate(place_order):
+            if place % 4 != group:
+                continue
             terms = terms + x_ref[source * 16 : source * 16 + 16, :].astype(F32)
         weight = 2.0
         if group == 0:
@@ -306,7 +307,7 @@
         [
             o * win_count + w + q
             for q in range(parts)
-            for o in turned(range(groups), first_owner)
+            for o in owner_order
         ]
         for w in range(0, win_count, parts)
     ]
@@ -329,7 +330,7 @@
         "win",
         split_axis=0,
         concat_axis=0,
-        axis_index_groups=[turned(range(win_count), first_place)],
+        axis_index_groups=[list(place_order)],
         tiled=True,
     ).reshape(win_count * 16, width)
     return call(

time: 47.9 us -> 47.3 us (0.987)
  no operation moved by 1% of the time
where the time goes in v5:
time: 47.3 us; the launch traced here: 47.1 us
  blocking collectives  42.3 us (89%)
  Pallas kernels  4.2 us (9%)
  between operations  0.67 us (1%)
    all_to_all x1, blocking collectives, body(): lax.all_to_all(terms.reshape(win_count, 16, width), 'win', split_axis=0,...  21.9 us
    all_to_all x1, blocking collectives, body(): lax.all_to_all(outgoing.reshape(parts * groups, per_group, width), ('chan...  20.4 us
    pallas_call x3, Pallas kernels, call(): pl.pallas_call(kernel, out_shape=out, in_specs=specs or [VMEM] * len(oper...  4.2 us

profile of v5, /device:TPU:1, one launch (start us, length us, event | category | flops | bytes accessed | tf_op | source)
XLA Modules:
  0.0 47.1 jit_solution(17140950995453162249)
XLA Ops:
  0.7 2.5 %shard_map.64 = (bf16[4,384,128]{2,1,0:T(8,128)(2,1)S(1)}, bf16[2,4,256,256]{3,2,1,0:T(8,128)(2,1)S(1)}, s32[192,1]{1,0:T(8,128)S(1)}, f32[8,128]{1,0:T(8,128)S(1)}) custom-call(s32[1]{0:T(128)} %bitcast.owner_ref, s32[1]{0:T(128)} %bitcast.1.place_ref, s32[1]{0:T(128)S(6)} %copy.7.live_ref, f32[64,2,1024]{2,1,0:T(2,128)} %x_hbm.1, ...), custom_call_target="tpu_custom_call" | custom-call | tf_op jit(solution)/shard_map/pallas_call | solution.py:260
  3.2 20.4 %all_to_all.10 = bf16[64,24,128]{2,1,0:T(8,128)(2,1)S(1)} all-to-all(bf16[64,24,128]{2,1,0:T(8,128)(2,1)S(1)} %bitcast.9), channel_id=1, replica_groups={{320,352,384,416,448,480,0,32,64,96,128,160,192,224,256,288,321,353,385..., dimensions={0} | all-to-all | bytes 786432 | tf_op jit(solution)/shard_map/all_to_all | solution.py:314
  23.6 0.7 %shard_map.65 = bf16[512,128]{1,0:T(8,128)(2,1)S(1)} custom-call(bf16[4,384,128]{2,1,0:T(8,128)(2,1)S(1)} %bitcast.6, s32[192,1]{1,0:T(8,128)S(1)} %get-tuple-element.10.index_ref), custom_call_target="tpu_custom_call" | custom-call | tf_op jit(solution)/shard_map/pallas_call | solution.py:260
  24.2 21.9 %all_to_all.11 = bf16[32,16,128]{2,1,0:T(8,128)(2,1)S(1)} all-to-all(bf16[32,16,128]{2,1,0:T(8,128)(2,1)S(1)} %bitcast.8), channel_id=1, replica_groups={{20,21,2,3,16,17,30,31,12,13,26,27,8,9,22,23,4,5,18,19,0,1,14,15,28,29,..., dimensions={0} | all-to-all | bytes 262144 | tf_op jit(solution)/shard_map/all_to_all | solution.py:328
  46.1 1.0 %shard_map.66 = f32[8,1024]{1,0:T(8,128)} custom-call(bf16[512,128]{1,0:T(8,128)(2,1)S(1)} %bitcast.7, bf16[2,4,256,256]{3,2,1,0:T(8,128)(2,1)S(1)} %get-tuple-element.11.table_ref, f32[8,128]{1,0:T(8,128)S(1)} %get-tuple-element.12.scale_ref), custom_call_target="tpu_custom_call" | custom-call | tf_op jit(solution)/shard_map/pallas_call | solution.py:260

commit v6 on v5

--- a/solution.py
+++ b/solution.py
@@ -40,15 +40,11 @@
     return jnp.dot(a, b, preferred_element_type=F32)
 
 
-def dot_back(a, b):
-    return lax.dot_general(a, b, (((1,), (1,)), ((), ())), preferred_element_type=F32)
-
-
-def product(x, table_top, table_rest, by=dot):
+def product(x, table_top, table_rest):
     rows = x.shape[0]
     top, rest = split(x)
-    both = by(jnp.concatenate([top, rest], axis=0), table_top)
-    return both[:rows] + both[rows:] + by(top, table_rest)
+    both = dot(jnp.concatenate([top, rest], axis=0), table_top)
+    return both[:rows] + both[rows:] + dot(top, table_rest)
 
 
 def iota(shape, axis):
@@ -129,9 +125,9 @@
 
 
 def spectra_kernel(
-    owner_ref, place_ref, live_ref, x_hbm, table_hbm, needed_hbm, homes_hbm, partners_hbm,
-    out_ref, table_ref, pick_ref, scale_ref,
-    x_ref, needed_ref, homes_ref, partners_ref, band_ref, sems,
+    owner_ref, place_ref, live_ref, x_hbm, table_hbm, back_hbm, needed_hbm, homes_hbm, partners_hbm,
+    out_ref, back_ref, pick_ref, scale_ref,
+    x_ref, table_ref, needed_ref, homes_ref, partners_ref, band_ref, sems,
 ):
     channels, windows, samples = x_ref.shape
     quarter = samples // 4
@@ -147,6 +143,9 @@
     for group in range(4):
         for level in range(2):
             pairs.append((table_hbm.at[level, group], table_ref.at[level, group]))
+    last = len(pairs)
+    for level in range(2):
+        pairs.append((back_hbm.at[level], back_ref.at[level]))
     copies = [pltpu.make_async_copy(*pair, sems.at[i]) for i, pair in enumerate(pairs)]
     for copy in copies:
         copy.start()
@@ -157,12 +156,13 @@
         copy.wait()
     chosen = one_hot(send_rows(needed_ref[...], owner_ref[0], channels), 4 * channels)
     listed = needed_ref[pl.ds(owner_ref[0], 1), :]
-    pick_ref[...] = pick_rows(listed, homes_ref[...], partners_ref[...], owners, channels)
+    picks = pick_rows(listed, homes_ref[...], partners_ref[...], owners, channels)
+    pick_ref[...] = one_hot(picks, pick_ref.shape[1])
     live = lax.div(place_ref[0], 16) < live_ref[0]
     scale = jnp.where(live, 1.0 / math.sqrt(samples * 64), 0.0)
     scale_ref[...] = jnp.full(scale_ref.shape, scale, F32)
 
-    for copy in copies[3:]:
+    for copy in copies[3:last]:
         copy.wait()
     x = jnp.concatenate([x_ref[:, w, :] for w in range(windows)], axis=0)
     rows = x.shape[0]
@@ -194,12 +194,14 @@
     width = out_ref.shape[2]
     for part in range(out_ref.shape[0]):
         out_ref[part] = picked[:, part * width : (part + 1) * width]
-
-
-def cross_kernel(x_ref, index_ref, out_ref, held_ref):
-    parts, rows, width = x_ref.shape
-    x = jnp.concatenate([x_ref[part] for part in range(parts)], axis=1)
-    held_ref[...] = dot(one_hot(index_ref[...], rows), x)
+    for copy in copies[last:]:
+        copy.wait()
+
+
+def cross_kernel(x_ref, pick_ref, out_ref, held_ref):
+    parts, _, width = x_ref.shape
+    for part in range(parts):
+        held_ref[:, part * width : (part + 1) * width] = dot(pick_ref[...], x_ref[part])
     for block in range(2):
         cr, ci = [0.0] * 8, [0.0] * 8
         for window in range(2):
@@ -241,7 +243,7 @@
         side = jnp.concatenate([cr, -ci], axis=1)
         if group >= 2:
             side = jnp.concatenate([side, jnp.concatenate([ci, cr], axis=1)], axis=0)
-        waves.append(product(side, table_ref[0, group], table_ref[1, group], dot_back))
+        waves.append(product(side, table_ref[0, group], table_ref[1, group]))
     a0, a2, b1, b3 = waves
     plus, minus = a0 + a2, a0 - a2
     cos = b1[:8] + b3[:8]
@@ -282,25 +284,26 @@
     table = wave_tables(samples)
     far = [
         pltpu.with_memory_space_constraint(jnp.asarray(a), pltpu.HBM)
-        for a in (traces, table, needed, home_slot, partner_slot)
+        for a in (traces, table, table.swapaxes(2, 3), needed, home_slot, partner_slot)
     ]
     outgoing, waves, pick, scale = call(
         spectra_kernel,
         [
             jax.ShapeDtypeStruct((parts, groups * per_group, width), BF16),
             jax.ShapeDtypeStruct(table.shape, BF16),
-            jax.ShapeDtypeStruct((held_rows, 1), I32),
+            jax.ShapeDtypeStruct((held_rows, groups * per_group), BF16),
             jax.ShapeDtypeStruct((8, 128), F32),
         ],
         (owner[None], place[None], live_blocks, *far),
         [SMEM, SMEM, SMEM] + [HBM] * len(far),
         [
             pltpu.VMEM(traces.shape, F32),
+            pltpu.VMEM(table.shape, BF16),
             pltpu.VMEM(needed.shape, I32),
             pltpu.VMEM(home_slot.shape, I32),
             pltpu.VMEM(partner_slot.shape, I32),
             pltpu.VMEM((bins, bins), BF16),
-            pltpu.SemaphoreType.DMA((13,)),
+            pltpu.SemaphoreType.DMA((15,)),
         ],
     )
     near = [

time: 47.3 us -> 47.1 us (level)
  no operation moved by 1% of the time
where the time goes in v6:
time: 47.1 us; the launch traced here: 46.9 us
  blocking collectives  42.2 us (90%)
  Pallas kernels  3.95 us (8%)
  between operations  0.67 us (1%)
    all_to_all x1, blocking collectives, body(): lax.all_to_all(terms.reshape(win_count, 16, width), 'win', split_axis=0,...  21.8 us
    all_to_all x1, blocking collectives, body(): lax.all_to_all(outgoing.reshape(parts * groups, per_group, width), ('chan...  20.4 us
    pallas_call x3, Pallas kernels, call(): pl.pallas_call(kernel, out_shape=out, in_specs=specs or [VMEM] * len(oper...  3.95 us

profile of v6, /device:TPU:1, one launch (start us, length us, event | category | flops | bytes accessed | tf_op | source)
XLA Modules:
  0.0 46.9 jit_solution(2619014011457692573)
XLA Ops:
  0.7 2.5 %shard_map.73 = (bf16[4,384,128]{2,1,0:T(8,128)(2,1)S(1)}, bf16[2,4,256,256]{3,2,1,0:T(8,128)(2,1)S(1)}, bf16[192,384]{1,0:T(8,128)(2,1)S(1)}, f32[8,128]{1,0:T(8,128)S(1)}) custom-call(s32[1]{0:T(128)} %bitcast.owner_ref, s32[1]{0:T(128)} %bitcast.1.place_ref, s32[1]{0:T(128)S(6)} %copy.8.live_ref, f32[64,2,1024]{2,1,0:T(2,128)} %x_hbm.1, ...), custom_call_target="tpu_custom_call" | custom-call | tf_op jit(solution)/shard_map/pallas_call | solution.py:262
  3.2 20.4 %all_to_all.10 = bf16[64,24,128]{2,1,0:T(8,128)(2,1)S(1)} all-to-all(bf16[64,24,128]{2,1,0:T(8,128)(2,1)S(1)} %bitcast.9), channel_id=1, replica_groups={{320,352,384,416,448,480,0,32,64,96,128,160,192,224,256,288,321,353,385..., dimensions={0} | all-to-all | bytes 786432 | tf_op jit(solution)/shard_map/all_to_all | solution.py:317
  23.6 0.5 %shard_map.74 = bf16[512,128]{1,0:T(8,128)(2,1)S(1)} custom-call(bf16[4,384,128]{2,1,0:T(8,128)(2,1)S(1)} %bitcast.6, bf16[192,384]{1,0:T(8,128)(2,1)S(1)} %get-tuple-element.10.pick_ref), custom_call_target="tpu_custom_call" | custom-call | tf_op jit(solution)/shard_map/pallas_call | solution.py:262
  24.1 21.8 %all_to_all.11 = bf16[32,16,128]{2,1,0:T(8,128)(2,1)S(1)} all-to-all(bf16[32,16,128]{2,1,0:T(8,128)(2,1)S(1)} %bitcast.8), channel_id=1, replica_groups={{20,21,2,3,16,17,30,31,12,13,26,27,8,9,22,23,4,5,18,19,0,1,14,15,28,29,..., dimensions={0} | all-to-all | bytes 262144 | tf_op jit(solution)/shard_map/all_to_all | solution.py:331
  46.0 0.9 %shard_map.75 = f32[8,1024]{1,0:T(8,128)} custom-call(bf16[512,128]{1,0:T(8,128)(2,1)S(1)} %bitcast.7, bf16[2,4,256,256]{3,2,1,0:T(8,128)(2,1)S(1)} %get-tuple-element.11.table_ref, f32[8,128]{1,0:T(8,128)S(1)} %get-tuple-element.12.scale_ref), custom_call_target="tpu_custom_call" | custom-call | tf_op jit(solution)/shard_map/pallas_call | solution.py:262

commit v7 on v6

--- a/solution.py
+++ b/solution.py
@@ -12,6 +12,7 @@
 band_reach = 64
 bin_groups = (0, 2, 1, 3)
 owner_order = tuple((10 + i) % 16 for i in range(16))
+quarter_order = (1, 0, 3, 2)
 place_order = (20, 21, 2, 3, 16, 17, 30, 31, 12, 13, 26, 27, 8, 9, 22, 23, 4, 5, 18, 19, 0, 1, 14, 15, 28, 29, 10, 11, 24, 25, 6, 7)
 F32 = jnp.float32
 BF16 = jnp.bfloat16
@@ -192,8 +193,8 @@
     white = jnp.concatenate([(re * factor).astype(BF16), (im * factor).astype(BF16)], axis=0)
     picked = dot(chosen, white).astype(BF16)
     width = out_ref.shape[2]
-    for part in range(out_ref.shape[0]):
-        out_ref[part] = picked[:, part * width : (part + 1) * width]
+    for spot, part in enumerate(quarter_order):
+        out_ref[spot] = picked[:, part * width : (part + 1) * width]
     for copy in copies[last:]:
         copy.wait()
 
@@ -309,7 +310,7 @@
     near = [
         [
             o * win_count + w + q
-            for q in range(parts)
+            for q in quarter_order
             for o in owner_order
         ]
         for w in range(0, win_count, parts)

time: 47.1 us -> 46.7 us (level)
  no operation moved by 1% of the time
where the time goes in v7:
time: 46.7 us; the launch traced here: 46.5 us
  blocking collectives  41.9 us (90%)
  Pallas kernels  3.94 us (8%)
  between operations  0.67 us (1%)
    all_to_all x1, blocking collectives, body(): lax.all_to_all(terms.reshape(win_count, 16, width), 'win', split_axis=0,...  22 us
    all_to_all x1, blocking collectives, body(): lax.all_to_all(outgoing.reshape(parts * groups, per_group, width), ('chan...  19.9 us
    pallas_call x3, Pallas kernels, call(): pl.pallas_call(kernel, out_shape=out, in_specs=specs or [VMEM] * len(oper...  3.94 us

profile of v7, /device:TPU:1, one launch (start us, length us, event | category | flops | bytes accessed | tf_op | source)
XLA Modules:
  0.0 46.5 jit_solution(16584498805070268635)
XLA Ops:
  0.7 2.5 %shard_map.73 = (bf16[4,384,128]{2,1,0:T(8,128)(2,1)S(1)}, bf16[2,4,256,256]{3,2,1,0:T(8,128)(2,1)S(1)}, bf16[192,384]{1,0:T(8,128)(2,1)S(1)}, f32[8,128]{1,0:T(8,128)S(1)}) custom-call(s32[1]{0:T(128)} %bitcast.owner_ref, s32[1]{0:T(128)} %bitcast.1.place_ref, s32[1]{0:T(128)S(6)} %copy.8.live_ref, f32[64,2,1024]{2,1,0:T(2,128)} %x_hbm.1, ...), custom_call_target="tpu_custom_call" | custom-call | tf_op jit(solution)/shard_map/pallas_call | solution.py:263
  3.2 19.9 %all_to_all.10 = bf16[64,24,128]{2,1,0:T(8,128)(2,1)S(1)} all-to-all(bf16[64,24,128]{2,1,0:T(8,128)(2,1)S(1)} %bitcast.9), channel_id=1, replica_groups={{321,353,385,417,449,481,1,33,65,97,129,161,193,225,257,289,320,352,384..., dimensions={0} | all-to-all | bytes 786432 | tf_op jit(solution)/shard_map/all_to_all | solution.py:318
  23.1 0.5 %shard_map.74 = bf16[512,128]{1,0:T(8,128)(2,1)S(1)} custom-call(bf16[4,384,128]{2,1,0:T(8,128)(2,1)S(1)} %bitcast.6, bf16[192,384]{1,0:T(8,128)(2,1)S(1)} %get-tuple-element.10.pick_ref), custom_call_target="tpu_custom_call" | custom-call | tf_op jit(solution)/shard_map/pallas_call | solution.py:263
  23.7 22.0 %all_to_all.11 = bf16[32,16,128]{2,1,0:T(8,128)(2,1)S(1)} all-to-all(bf16[32,16,128]{2,1,0:T(8,128)(2,1)S(1)} %bitcast.8), channel_id=1, replica_groups={{20,21,2,3,16,17,30,31,12,13,26,27,8,9,22,23,4,5,18,19,0,1,14,15,28,29,..., dimensions={0} | all-to-all | bytes 262144 | tf_op jit(solution)/shard_map/all_to_all | solution.py:332
  45.6 0.9 %shard_map.75 = f32[8,1024]{1,0:T(8,128)} custom-call(bf16[512,128]{1,0:T(8,128)(2,1)S(1)} %bitcast.7, bf16[2,4,256,256]{3,2,1,0:T(8,128)(2,1)S(1)} %get-tuple-element.11.table_ref, f32[8,128]{1,0:T(8,128)S(1)} %get-tuple-element.12.scale_ref), custom_call_target="tpu_custom_call" | custom-call | tf_op jit(solution)/shard_map/pallas_call | solution.py:263

commit v8 on v7

--- a/solution.py
+++ b/solution.py
@@ -11,7 +11,7 @@
 
 band_reach = 64
 bin_groups = (0, 2, 1, 3)
-owner_order = tuple((10 + i) % 16 for i in range(16))
+owner_order = tuple((10 + 7 * i) % 16 for i in range(16))
 quarter_order = (1, 0, 3, 2)
 place_order = (20, 21, 2, 3, 16, 17, 30, 31, 12, 13, 26, 27, 8, 9, 22, 23, 4, 5, 18, 19, 0, 1, 14, 15, 28, 29, 10, 11, 24, 25, 6, 7)
 F32 = jnp.float32

time: 46.7 us -> 46.7 us (level)
  no operation moved by 1% of the time
where the time goes in v8:
time: 46.7 us; the launch traced here: 46.5 us
  blocking collectives  41.9 us (90%)
  Pallas kernels  3.95 us (8%)
  between operations  0.67 us (1%)
    all_to_all x1, blocking collectives, body(): lax.all_to_all(terms.reshape(win_count, 16, width), 'win', split_axis=0,...  21.8 us
    all_to_all x1, blocking collectives, body(): lax.all_to_all(outgoing.reshape(parts * groups, per_group, width), ('chan...  20 us
    pallas_call x3, Pallas kernels, call(): pl.pallas_call(kernel, out_shape=out, in_specs=specs or [VMEM] * len(oper...  3.95 us

profile of v8, /device:TPU:1, one launch (start us, length us, event | category | flops | bytes accessed | tf_op | source)
XLA Modules:
  0.0 46.5 jit_solution(16358656466726950397)
XLA Ops:
  0.7 2.5 %shard_map.73 = (bf16[4,384,128]{2,1,0:T(8,128)(2,1)S(1)}, bf16[2,4,256,256]{3,2,1,0:T(8,128)(2,1)S(1)}, bf16[192,384]{1,0:T(8,128)(2,1)S(1)}, f32[8,128]{1,0:T(8,128)S(1)}) custom-call(s32[1]{0:T(128)} %bitcast.owner_ref, s32[1]{0:T(128)} %bitcast.1.place_ref, s32[1]{0:T(128)S(6)} %copy.8.live_ref, f32[64,2,1024]{2,1,0:T(2,128)} %x_hbm.1, ...), custom_call_target="tpu_custom_call" | custom-call | tf_op jit(solution)/shard_map/pallas_call | solution.py:263
  3.2 20.0 %all_to_all.10 = bf16[64,24,128]{2,1,0:T(8,128)(2,1)S(1)} all-to-all(bf16[64,24,128]{2,1,0:T(8,128)(2,1)S(1)} %bitcast.9), channel_id=1, replica_groups={{321,33,257,481,193,417,129,353,65,289,1,225,449,161,385,97,320,32,256,..., dimensions={0} | all-to-all | bytes 786432 | tf_op jit(solution)/shard_map/all_to_all | solution.py:318
  23.2 0.5 %shard_map.74 = bf16[512,128]{1,0:T(8,128)(2,1)S(1)} custom-call(bf16[4,384,128]{2,1,0:T(8,128)(2,1)S(1)} %bitcast.6, bf16[192,384]{1,0:T(8,128)(2,1)S(1)} %get-tuple-element.10.pick_ref), custom_call_target="tpu_custom_call" | custom-call | tf_op jit(solution)/shard_map/pallas_call | solution.py:263
  23.8 21.8 %all_to_all.11 = bf16[32,16,128]{2,1,0:T(8,128)(2,1)S(1)} all-to-all(bf16[32,16,128]{2,1,0:T(8,128)(2,1)S(1)} %bitcast.8), channel_id=1, replica_groups={{20,21,2,3,16,17,30,31,12,13,26,27,8,9,22,23,4,5,18,19,0,1,14,15,28,29,..., dimensions={0} | all-to-all | bytes 262144 | tf_op jit(solution)/shard_map/all_to_all | solution.py:332
  45.6 0.9 %shard_map.75 = f32[8,1024]{1,0:T(8,128)} custom-call(bf16[512,128]{1,0:T(8,128)(2,1)S(1)} %bitcast.7, bf16[2,4,256,256]{3,2,1,0:T(8,128)(2,1)S(1)} %get-tuple-element.11.table_ref, f32[8,128]{1,0:T(8,128)S(1)} %get-tuple-element.12.scale_ref), custom_call_target="tpu_custom_call" | custom-call | tf_op jit(solution)/shard_map/pallas_call | solution.py:263
